TPU v7x, 512 devices: a whole 4x8x8 slice. The times are simulated.
512 devices in a mesh: light: 4 (over x_lo, core), strip: 128 (over z, y, x_hi).
Axes of the slice: x: 4 (x_hi: 2, x_lo: 2; x = x_hi * 2 + x_lo), y: 8, z: 8, core: 2. Of those that a mesh axis runs over, the one named last changes fastest.
Arguments:
- depth_start: float32 [128, 65536], P(None, 'strip'), may hold values from -0.3 to 0.3
- albedo_start: float32 [128, 65536], P(None, 'strip'), may hold values from 0.5 to 2
- observations: bfloat16 [32, 128, 65536], P('light', None, 'strip'), may hold values from 0 to 26
- light_table: int32 [32, 4], P('light'), may hold values from 0 to 999
- valid_mask: int32 [128, 65536], P(None, 'strip'), may hold values 0 or 1
Outputs:
- depth_final: float32 [128, 65536], P(None, 'strip')
- albedo_final: float32 [128, 65536], P(None, 'strip')
All inputs are finite; a program needn't handle non-finite values. No bound on the sum of `valid_mask` on one device may be relied on, other than what follows from the above.
Results may differ from a plain program's by a relative error of at most 0.0003.
Values may be sent and summed in bfloat16 or wider, within the bound.
A program may use at most 64 MiB of HBM per device.

v0:
```python
import jax
import jax.numpy as jnp
from jax import lax
from jax.sharding import PartitionSpec as P

ITERS = 2


temper = 0.5
step_depth = 0.1
step_albedo = 0.2
epsilon = 1e-06


def extended(block, sides, width):
    for axis, dim in sides:
        count = lax.axis_size(axis)
        forward = [(i, i + 1) for i in range(count - 1)]
        backward = [(target, source) for source, target in forward]
        low = lax.ppermute(
            lax.slice_in_dim(block, block.shape[dim] - width, None, axis=dim), axis, forward
        )
        high = lax.ppermute(lax.slice_in_dim(block, 0, width, axis=dim), axis, backward)
        block = jnp.concatenate([low, block, high], axis=dim)
    return block


def decode_lights(table):
    values = table.astype(jnp.float32)
    light_x = (values[:, 0] / 500.0 - 1.0)[:, None, None]
    light_y = (values[:, 1] / 500.0 - 1.0)[:, None, None]
    light_z = (1.0 + values[:, 2] / 1000.0)[:, None, None]
    intensity = (0.5 + values[:, 3] / 1000.0)[:, None, None]
    return (light_x, light_y, light_z, intensity)


def shade_terms(surface, col_pad, row_pad, albedo, observed, table, valid, coord_x, coord_y):
    slope_x = 0.5 * (col_pad[:, 2:] - col_pad[:, :-2])
    slope_y = 0.5 * (row_pad[2:] - row_pad[:-2])
    light_x, light_y, light_z, intensity = decode_lights(table)
    delta_x = light_x - coord_x
    delta_y = light_y - coord_y
    delta_z = light_z - surface
    distance_sq = delta_x * delta_x + delta_y * delta_y + delta_z * delta_z
    norm_sq = 1.0 + slope_x * slope_x + slope_y * slope_y
    facing = -slope_x * delta_x - slope_y * delta_y + delta_z
    falloff = intensity / (distance_sq * jnp.sqrt(distance_sq) * jnp.sqrt(norm_sq))
    radiance = albedo * falloff * facing
    residual = valid * (radiance - observed.astype(jnp.float32))
    scores = -temper * residual * residual
    return (
        scores,
        residual,
        falloff,
        facing,
        delta_x,
        delta_y,
        delta_z,
        distance_sq,
        norm_sq,
        slope_x,
        slope_y,
    )


def light_gradients(weights, terms, albedo):
    (
        scores,
        residual,
        falloff,
        facing,
        delta_x,
        delta_y,
        delta_z,
        distance_sq,
        norm_sq,
        slope_x,
        slope_y,
    ) = terms
    lit = weights * residual * falloff
    grad_albedo = jnp.sum(lit * facing, axis=0)
    scaled = lit * albedo
    grad_direct = jnp.sum(scaled * (-1.0 + 3.0 * facing * delta_z / distance_sq), axis=0)
    grad_x = jnp.sum(scaled * (-delta_x - facing * slope_x / norm_sq), axis=0)
    grad_y = jnp.sum(scaled * (-delta_y - facing * slope_y / norm_sq), axis=0)
    return (grad_x, grad_y, grad_direct, grad_albedo)


def depth_stencil(grad_x_pad, grad_y_pad, grad_direct):
    return (
        grad_direct
        + 0.5 * (grad_x_pad[:, :-2] - grad_x_pad[:, 2:])
        + 0.5 * (grad_y_pad[:-2] - grad_y_pad[2:])
    )


def coordinates(nrows, total_rows, strip_cols):
    total_cols = strip_cols * lax.axis_size("strip")
    col_start = lax.axis_index("strip") * strip_cols
    columns = (jnp.arange(strip_cols) + col_start).astype(jnp.float32)
    coord_x = ((columns + 0.5) / total_cols - 0.5)[None, :]
    row_index = jnp.arange(nrows).astype(jnp.float32)
    coord_y = ((row_index + 0.5 - total_rows / 2.0) / total_cols)[:, None]
    return (coord_x, coord_y)


def update(surface, albedo, full_depth, full_albedo, mean_depth, mean_albedo):
    surface = surface - step_depth * jnp.tanh(full_depth / jnp.sqrt(mean_depth + epsilon))
    albedo = albedo - step_albedo * jnp.tanh(full_albedo / jnp.sqrt(mean_albedo + epsilon))
    return (surface, albedo)


def shards(depth_start, albedo_start, observations, light_table, valid_mask):
    strip_cols = depth_start.shape[1]
    total_rows = depth_start.shape[0]
    surface = depth_start
    albedo = albedo_start
    valid = valid_mask.astype(jnp.float32)
    coord_x, coord_y = coordinates(total_rows, total_rows, strip_cols)
    for iteration in range(ITERS):
        col_pad = extended(surface, (("strip", 1),), 1)
        row_pad = jnp.pad(surface, ((1, 1), (0, 0)))
        terms = shade_terms(
            surface, col_pad, row_pad, albedo, observations, light_table, valid, coord_x, coord_y
        )
        scores = terms[0]
        local_high = jnp.max(scores, axis=0)
        highest = lax.pmax(local_high, "light")
        raised = jnp.exp(scores - highest)
        summed = lax.psum(jnp.sum(raised, axis=0), "light")
        weights = raised / summed
        grad_x, grad_y, grad_direct, grad_albedo = light_gradients(weights, terms, albedo)
        grad_x, grad_y, grad_direct, full_albedo = lax.psum(
            (grad_x, grad_y, grad_direct, grad_albedo), "light"
        )
        slope_pad = extended(grad_x, (("strip", 1),), 1)
        full_depth = depth_stencil(slope_pad, jnp.pad(grad_y, ((1, 1), (0, 0))), grad_direct)
        square_depth, square_albedo = lax.psum(
            (jnp.sum(full_depth * full_depth), jnp.sum(full_albedo * full_albedo)), "strip"
        )
        pixel_count = full_depth.size * lax.axis_size("strip")
        surface, albedo = update(
            surface,
            albedo,
            full_depth,
            full_albedo,
            square_depth / pixel_count,
            square_albedo / pixel_count,
        )
    return (surface, albedo)


def solution(mesh):
    in_specs = (
        P(None, "strip"),
        P(None, "strip"),
        P("light", None, "strip"),
        P("light", None),
        P(None, "strip"),
    )
    out_specs = (P(None, "strip"), P(None, "strip"))
    return jax.shard_map(shards, mesh=mesh, in_specs=in_specs, out_specs=out_specs, check_vma=False)
```

profile of v0, /device:TPU:256, one launch (start us, length us, event | category | flops | bytes accessed | tf_op | source)
XLA Modules:
  0.0 1122.0 jit_solution(17285056990642368736)
XLA Ops:
  8.3 6.9 collective-permute-start
  19.1 8.0 collective-permute-done.1
  27.1 2.4 fusion.45
  30.2 2.7 fusion.15
  33.1 42.2 %all-reduce.15.cloned.1.call-done = f32[128,512]{1,0:T(8,128)} async-done(((f32[128,512]{1,0:T(8,128)}), f32[128,512]{1,0:T(8,128)}) %all-reduce.15.cloned.1.call-update) | async-done | bytes 262160 | tf_op jit(solution)/shard_map/pmax | solution.py:128
  75.3 2.1 fusion.14
  77.4 48.5 %all-reduce.17.cloned.1.call-done = f32[128,512]{1,0:T(8,128)} async-done(((f32[128,512]{1,0:T(8,128)}), f32[128,512]{1,0:T(8,128)}) %all-reduce.17.cloned.1.call-update) | async-done | bytes 262160 | tf_op jit(solution)/shard_map/psum | solution.py:130
  126.0 5.8 multiply_reduce_fusion.5
  131.8 53.8 %all-reduce.25.cloned.1.call-done = (f32[128,512]{1,0:T(8,128)}, f32[128,512]{1,0:T(8,128)}, f32[128,512]{1,0:T(8,128)}, f32[128,512]{1,0:T(8,128)}) async-done(((f32[128,512]{1,0:T(8,128)}, f32[128,512]{1,0:T(8,128)}, f32[128,512]{1,0:T(8,128)}, f32[128,512]{1,0:T(8,128)}), (f32[128,512]{1,0:T(8,128)}, f32[128,512]{1,0:T(8,128)}, f32[128,512]{1,0:T(8,128)}, ...) | async-done | bytes 1048592 | tf_op jit(solution)/shard_map/psum | solution.py:133
  186.6 4.6 collective-permute-start.2
  191.2 7.0 collective-permute-start.3
  200.1 2.1 multiply_reduce_fusion.9
  202.2 360.2 %all-reduce.5 = (f32[]{:T(128)}, f32[]{:T(128)}) all-reduce(f32[]{:T(128)} %get-tuple-element.30, f32[]{:T(128)} %multiply_reduce_fusion.8), channel_id=1, replica_groups=mesh['light'=4,'strip'=128] {'strip'}, use_global_device_ids=true, to_apply=%region_11.12 | all-reduce | flops 2 | bytes 16 | tf_op jit(solution)/shard_map/psum | solution.py:138
  565.9 5.4 collective-permute-start.5
  571.6 6.1 collective-permute-done.5
  579.4 4.0 fusion.17
  583.5 41.5 %all-reduce.19.cloned.1.call-done = f32[128,512]{1,0:T(8,128)} async-done(((f32[128,512]{1,0:T(8,128)}), f32[128,512]{1,0:T(8,128)}) %all-reduce.19.cloned.1.call-update) | async-done | bytes 262160 | tf_op jit(solution)/shard_map/pmax | solution.py:128
  627.1 48.4 %all-reduce.21.cloned.1.call-done = f32[128,512]{1,0:T(8,128)} async-done(((f32[128,512]{1,0:T(8,128)}), f32[128,512]{1,0:T(8,128)}) %all-reduce.21.cloned.1.call-update) | async-done | bytes 262160 | tf_op jit(solution)/shard_map/psum | solution.py:130
  675.5 5.7 multiply_reduce_fusion.2
  681.3 53.9 %all-reduce.23.cloned.1.call-done = (f32[128,512]{1,0:T(8,128)}, f32[128,512]{1,0:T(8,128)}, f32[128,512]{1,0:T(8,128)}, f32[128,512]{1,0:T(8,128)}) async-done(((f32[128,512]{1,0:T(8,128)}, f32[128,512]{1,0:T(8,128)}, f32[128,512]{1,0:T(8,128)}, f32[128,512]{1,0:T(8,128)}), (f32[128,512]{1,0:T(8,128)}, f32[128,512]{1,0:T(8,128)}, f32[128,512]{1,0:T(8,128)}, ...) | async-done | bytes 1048592 | tf_op jit(solution)/shard_map/psum | solution.py:133
  736.1 4.6 collective-permute-start.6
  740.7 7.0 collective-permute-start.7
  749.5 2.1 multiply_reduce_fusion.7
  751.7 360.2 %all-reduce.4 = (f32[]{:T(128)}, f32[]{:T(128)}) all-reduce(f32[]{:T(128)} %get-tuple-element.22, f32[]{:T(128)} %multiply_reduce_fusion.6), channel_id=1, replica_groups=mesh['light'=4,'strip'=128] {'strip'}, use_global_device_ids=true, to_apply=%region_27.28 | all-reduce | flops 2 | bytes 16 | tf_op jit(solution)/shard_map/psum | solution.py:138
  (74 shorter events, 19.5 us)
Async XLA Ops:
  7.2 23.0 %copy-start = (f32[128,512]{1,0:T(8,128)S(1)}, f32[128,512]{1,0:T(8,128)}, u32[]{:S(2)}) copy-start(f32[128,512]{1,0:T(8,128)} %param.5) | copy-start | bytes 786436
  7.2 23.0 %copy-start.1 = (bf16[8,128,512]{2,1,0:T(8,128)(2,1)S(1)}, bf16[8,128,512]{2,1,0:T(8,128)(2,1)}, u32[]{:S(2)}) copy-start(bf16[8,128,512]{2,1,0:T(8,128)(2,1)} %param.7) | copy-start | bytes 3145732
  7.2 68.1 %all-reduce.15.cloned.1.call-start = ((), (), s32[]{:S(2)}) async-start(), calls=%async_computation | async-start | bytes 524288 | tf_op jit(solution)/shard_map/pmax | solution.py:128
  8.3 10.8 collective-permute-start
  15.2 11.9 %collective-permute-start.1 = (f32[128,1]{1,0:T(8,128)S(1)}, f32[128,1]{1,0:T(8,128)S(1)}, u32[]{:S(2)}, u32[]{:S(2)}) collective-permute-start(f32[128,1]{1,0:T(8,128)S(1)} %get-tuple-element.45), channel_id=1, source_target_pairs={{0,1},{1,2},{2,3},{3,4},{4,5},{5,6},{6,7},{7,8},{8,9},{9,10},{10,1... | collective-permute-start | bytes 1544 | tf_op jit(solution)/shard_map/ppermute | solution.py:20
  19.0 13.9 %copy-start.2 = (f32[128,512]{1,0:T(8,128)}, f32[128,512]{1,0:T(8,128)S(1)}, u32[]{:S(2)}) copy-start(f32[128,512]{1,0:T(8,128)S(1)} %convert_element_type.30) | copy-start | bytes 786436
  32.9 93.0 %copy-start.7 = (f32[128,512]{1,0:T(8,128)S(1)}, f32[128,512]{1,0:T(8,128)}, u32[]{:S(2)}) copy-start(f32[128,512]{1,0:T(8,128)} %param.6) | copy-start | bytes 786436
  32.9 93.0 %copy-start.5 = (f32[128,512]{1,0:T(8,128)S(1)}, f32[128,512]{1,0:T(8,128)}, u32[]{:S(2)}) copy-start(f32[128,512]{1,0:T(8,128)} %copy-done.4) | copy-start | bytes 786436
  33.0 93.0 %copy-start.11 = (f32[128,512]{1,0:T(8,128)S(1)}, f32[128,512]{1,0:T(8,128)}, u32[]{:S(2)}) copy-start(f32[128,512]{1,0:T(8,128)} %copy-done.10) | copy-start | bytes 786436
  33.0 93.0 %copy-start.13 = (f32[128,512]{1,0:T(8,128)S(1)}, f32[128,512]{1,0:T(8,128)}, u32[]{:S(2)}) copy-start(f32[128,512]{1,0:T(8,128)} %copy-done.12) | copy-start | bytes 786436
  33.0 93.0 %all-reduce.17.cloned.1.call-start = ((), (), s32[]{:S(2)}) async-start(), calls=%async_computation.1 | async-start | bytes 524288 | tf_op jit(solution)/shard_map/psum | solution.py:130
  77.4 108.3 %all-reduce.25.cloned.1.call-start = ((), (), s32[]{:S(2)}) async-start(), calls=%async_computation.5 | async-start | bytes 2097152 | tf_op jit(solution)/shard_map/psum | solution.py:133
  131.8 493.2 %all-reduce.19.cloned.1.call-start = ((), (), s32[]{:S(2)}) async-start(), calls=%async_computation.2 | async-start | bytes 524288 | tf_op jit(solution)/shard_map/pmax | solution.py:128
  185.6 385.7 %copy-start.16 = (f32[128,512]{1,0:T(8,128)S(1)}, f32[128,512]{1,0:T(8,128)}, u32[]{:S(2)}) copy-start(f32[128,512]{1,0:T(8,128)} %get-tuple-element.21) | copy-start | bytes 786436
  186.6 13.2 %collective-permute-start.2 = (f32[128,1]{1,0:T(8,128)S(1)}, f32[128,1]{1,0:T(8,128)S(1)}, u32[]{:S(2)}, u32[]{:S(2)}) collective-permute-start(f32[128,1]{1,0:T(8,128)S(1)} %get-tuple-element.42), channel_id=1, source_target_pairs={{0,1},{1,2},{2,3},{3,4},{4,5},{5,6},{6,7},{7,8},{8,9},{9,10},{10,1... | collective-permute-start | bytes 1544 | tf_op jit(solution)/shard_map/ppermute | solution.py:20
  191.2 8.9 collective-permute-start.3
  202.2 377.2 %copy-start.3 = (f32[128,512]{1,0:T(8,128)S(1)}, f32[128,512]{1,0:T(8,128)}, u32[]{:S(2)}) copy-start(f32[128,512]{1,0:T(8,128)} %copy-done.2) | copy-start | bytes 786436
  563.9 7.7 collective-permute-start.4
  565.9 11.9 %collective-permute-start.5 = (f32[128,1]{1,0:T(8,128)S(1)}, f32[128,1]{1,0:T(8,128)S(1)}, u32[]{:S(2)}, u32[]{:S(2)}) collective-permute-start(f32[128,1]{1,0:T(8,128)S(1)} %get-tuple-element.41), channel_id=1, source_target_pairs={{0,1},{1,2},{2,3},{3,4},{4,5},{5,6},{6,7},{7,8},{8,9},{9,10},{10,1... | collective-permute-start | bytes 1544 | tf_op jit(solution)/shard_map/ppermute | solution.py:20
  583.4 92.1 %copy-start.9 = (f32[128,512]{1,0:T(8,128)S(1)}, f32[128,512]{1,0:T(8,128)}, u32[]{:S(2)}) copy-start(f32[128,512]{1,0:T(8,128)} %copy-done.8) | copy-start | bytes 786436
  583.4 92.1 %all-reduce.21.cloned.1.call-start = ((), (), s32[]{:S(2)}) async-start(), calls=%async_computation.3 | async-start | bytes 524288 | tf_op jit(solution)/shard_map/psum | solution.py:130
  627.1 108.1 %all-reduce.23.cloned.1.call-start = ((), (), s32[]{:S(2)}) async-start(), calls=%async_computation.4 | async-start | bytes 2097152 | tf_op jit(solution)/shard_map/psum | solution.py:133
  736.1 13.2 %collective-permute-start.6 = (f32[128,1]{1,0:T(8,128)S(1)}, f32[128,1]{1,0:T(8,128)S(1)}, u32[]{:S(2)}, u32[]{:S(2)}) collective-permute-start(f32[128,1]{1,0:T(8,128)S(1)} %get-tuple-element.38), channel_id=1, source_target_pairs={{0,1},{1,2},{2,3},{3,4},{4,5},{5,6},{6,7},{7,8},{8,9},{9,10},{10,1... | collective-permute-start | bytes 1544 | tf_op jit(solution)/shard_map/ppermute | solution.py:20
  740.7 8.9 collective-permute-start.7
  (7 other events, 29.4 us)
Sparse Core Ops, SparseCore 0:
  33.1 42.0 all-reduce.14
  78.2 47.7 all-reduce.16
  131.9 53.6 all-reduce.24
  583.5 41.3 all-reduce.18
  627.7 47.7 all-reduce.20
  681.4 53.6 all-reduce.22
where the time goes:
time: 1120 us
  blocking collectives  720 us (64%)
  waiting for transfers between devices  303 us (27%)
  starting transfers between devices  39.6 us (4%)
  other arithmetic  37 us (3%)
  between operations  17.1 us (2%)
    psum x2, blocking collectives, shards(): lax.psum((jnp.sum(full_depth * full_depth), jnp.sum(full_albedo * full_al...  720 us
    psum x2, waiting for transfers between devices, shards(): lax.psum((grad_x, grad_y, grad_direct, grad_albedo), 'light')  108 us
    psum x2, waiting for transfers between devices, shards(): summed = lax.psum(jnp.sum(raised, axis=0), 'light')  96.9 us
    pmax x2, waiting for transfers between devices, shards(): highest = lax.pmax(local_high, 'light')  83.7 us
    ppermute x4, starting transfers between devices, extended(): lax.ppermute(lax.slice_in_dim(block, 0, width, axis=dim), axis, backward)  22.8 us
  transfers between devices with their start and end apart: 14, of which 11 were waited for; matrix products, arithmetic and copies ran while one was open for 0% of the time, Pallas kernels for 0%

commit v1 on v0

v1 whole, which is shorter than its diff:
```python
import functools
import math

import jax
import jax.numpy as jnp
from jax import lax
from jax.experimental import pallas as pl
from jax.experimental.pallas import tpu as pltpu
from jax.sharding import PartitionSpec as P

MESH = pl.DeviceIdType.MESH
ITERS = 2
step_depth = 0.1
step_albedo = 0.2
epsilon = 1e-06
LOG2E = 1.4426950408889634

UNIT_ROWS = 16
LANES = 128
f32 = jnp.float32


def remote(src, dst, send, recv, device):
    return pltpu.make_async_remote_copy(
        src_ref=src, dst_ref=dst, send_sem=send, recv_sem=recv, device_id=device, device_id_type=MESH
    )


def kernel(
    cfg,
    depth_hbm, albedo_hbm, obs_hbm, table_hbm, mask_hbm,
    depth_out, albedo_out,
    depth, albedo, mask, table, obs_all, tables, lights,
    dx2, c2, spad, gxpad, gypad, gd, pix,
    tt, ff, fp, gg,
    fd_all, ga_all, fd_side, sums,
    in_sem, ob_send, ob_recv, tb_send, tb_recv, sd_send, sd_recv,
    gx_send, gx_recv, gy_send, gy_recv, fs_send, fs_recv, fd_send, fd_recv, ar_send, ar_recv,
):
    NQ, NS, RQ, COLS, TOTAL, FACT = cfg
    nl = obs_hbm.shape[0]
    rows = depth_hbm.shape[0]
    ct = COLS // LANES
    nu = (RQ // UNIT_ROWS) * ct
    NL = NQ * nl
    q = lax.axis_index("light")
    s = lax.axis_index("strip")
    nz, ny, nx = FACT
    z, y, xh = s // (ny * nx), lax.rem(s, ny * nx) // nx, lax.rem(s, nx)
    mates = [(lax.rem(q + k, NQ), s) for k in (2, 3, 1)]
    right = (q, lax.rem(s + 1, NS))
    left = (q, lax.rem(s + NS - 1, NS))

    phases = [
        [(q, lax.rem(s + ny * nx * k, NS)) for k in range(1, nz)],
        [(q, z * (ny * nx) + lax.rem(y * nx + xh + nx * k, ny * nx)) for k in range(1, ny)],
        [
            (lax.rem(q + k, NQ), z * (ny * nx) + y * nx + lax.rem(xh + h, nx))
            for h in range(nx)
            for k in range(NQ)
            if (h, k) != (0, 0)
        ],
    ]
    slot = [z, y, q * nx + xh]
    counts = [nz, ny, NQ * nx]

    base = pl.multiple_of(q * RQ, RQ)
    ins = [
        pltpu.make_async_copy(depth_hbm, depth, in_sem.at[0]),
        pltpu.make_async_copy(albedo_hbm, albedo, in_sem.at[1]),
        pltpu.make_async_copy(mask_hbm, mask, in_sem.at[2]),
        pltpu.make_async_copy(table_hbm, table, in_sem.at[3]),
        pltpu.make_async_copy(
            obs_hbm.at[:, pl.ds(base, RQ), :], obs_all.at[pl.ds(q * nl, nl)], in_sem.at[4]
        ),
    ]
    for c in ins:
        c.start()

    barrier = pltpu.get_barrier_semaphore()
    partners = mates + [left, right] + [p for ph in phases for p in ph]
    for p in partners:
        pl.semaphore_signal(barrier, inc=1, device_id=p, device_id_type=MESH)
    pl.semaphore_wait(barrier, len(partners))

    ins[3].wait()
    tables[pl.ds(q, 1)] = jnp.zeros((1, nl, LANES), f32)
    tables[pl.ds(q, 1), :, 0:4] = table[...].astype(f32)[None]
    tb = []
    for j, p in enumerate(mates):
        c = remote(tables.at[q], tables.at[q], tb_send.at[j], tb_recv.at[j], p)
        c.start()
        tb.append(c)
    sd = [
        remote(
            depth_hbm.at[pl.ds(base, RQ), pl.ds(COLS - LANES, LANES)],
            spad.at[pl.ds(8, RQ), pl.ds(0, LANES)], sd_send.at[0], sd_recv.at[0], right,
        ),
        remote(
            depth_hbm.at[pl.ds(base, RQ), pl.ds(0, LANES)],
            spad.at[pl.ds(8, RQ), pl.ds(LANES + COLS, LANES)], sd_send.at[1], sd_recv.at[1], left,
        ),
    ]
    for c in sd:
        c.start()

    def unit_at(u):
        half, i = u // (nu // 2), lax.rem(u, nu // 2)
        row, k = i // (ct // 2), lax.rem(i, ct // 2)
        if ct == 4:
            col = k * (3 - 2 * half) + half
        else:
            col = half * (ct // 2) + k
        return pl.multiple_of(row * UNIT_ROWS, UNIT_ROWS), pl.multiple_of(col * LANES, LANES)

    def ob_copy(j, u):
        p = mates[j]
        r, c = unit_at(u)
        return remote(
            obs_hbm.at[:, pl.ds(pl.multiple_of(p[0] * RQ + r, UNIT_ROWS), UNIT_ROWS), pl.ds(c, LANES)],
            obs_all.at[pl.ds(q * nl, nl), pl.ds(r, UNIT_ROWS), pl.ds(c, LANES)],
            ob_send.at[j, u], ob_recv.at[j, u], p,
        )

    def send_obs(u, carry):
        for j in range(NQ - 1):
            ob_copy(j, u).start()
        return carry

    lax.fori_loop(0, nu, send_obs, 0)

    for c in tb:
        c.wait()
    tab = tables[...].reshape(NL, LANES)
    lx = tab[:, 0:1] / 500.0 - 1.0
    ly = tab[:, 1:2] / 500.0 - 1.0
    lz = 1.0 + tab[:, 2:3] / 1000.0
    le = 0.5 + tab[:, 3:4] / 1000.0
    for k, v in enumerate((lx, ly, lz, le)):
        lights[k] = jnp.broadcast_to(v, (NL, LANES))
    col_i = lax.broadcasted_iota(jnp.int32, (1, COLS), 1) + s * COLS
    px = (col_i.astype(f32) + 0.5) / TOTAL - 0.5
    row_i = lax.broadcasted_iota(jnp.int32, (RQ, 1), 0) + q * RQ
    py = (row_i.astype(f32) + 0.5 - rows / 2.0) / TOTAL
    d = lx - px
    for j in range(ct):
        v = d[:, j * LANES : (j + 1) * LANES]
        dx2[j] = v * v
    pyb = jnp.broadcast_to(py, (RQ, LANES))

    def make_c2(l, carry):
        dy = lights[1, pl.ds(l, 1), :] - pyb
        dy2 = dy * dy
        for j in range(ct):
            sl = pl.ds(j * LANES, LANES)
            c2[l, :, sl] = dy2 + dx2[j, pl.ds(l, 1), :]
        return carry

    lax.fori_loop(0, NL, make_c2, 0)

    for k in (0, 1, 2, 4):
        ins[k].wait()
    for c in sd:
        c.wait()

    top_r = pl.multiple_of(jnp.maximum(q * RQ - 8, 0), 8)
    bot_r = pl.multiple_of(jnp.minimum(q * RQ + RQ, rows - 8), 8)
    not_top = jnp.where(q == 0, 0.0, 1.0).astype(f32)
    not_bot = jnp.where(q == NQ - 1, 0.0, 1.0).astype(f32)
    not_left = jnp.where(s == 0, 0.0, 1.0).astype(f32)
    not_right = jnp.where(s == NS - 1, 0.0, 1.0).astype(f32)
    own = pl.ds(base, RQ)
    lt, mid, rt = pl.ds(0, LANES), pl.ds(LANES, COLS), pl.ds(LANES + COLS, LANES)

    def fill_surface(cur):
        spad[pl.ds(0, 8), mid] = cur[pl.ds(top_r, 8), :] * not_top
        spad[pl.ds(8, RQ), mid] = cur[own, :]
        spad[pl.ds(8 + RQ, 8), mid] = cur[pl.ds(bot_r, 8), :] * not_bot

    fill_surface(depth)
    spad[pl.ds(8, RQ), lt] = spad[pl.ds(8, RQ), lt] * not_left
    spad[pl.ds(8, RQ), rt] = spad[pl.ds(8, RQ), rt] * not_right

    width = COLS + 2 * LANES

    def shifted(ref):
        x = ref[...] if ref.shape[0] == RQ else ref[pl.ds(8, RQ), :]
        lo = pltpu.roll(x, 1, 1)[:, LANES : LANES + COLS]
        hi = pltpu.roll(x, width - 1, 1)[:, LANES : LANES + COLS]
        return lo, hi

    for it in range(ITERS):
        lo, hi = shifted(spad)
        sx = 0.5 * (hi - lo)
        sy = 0.5 * (spad[pl.ds(9, RQ), mid] - spad[pl.ds(7, RQ), mid])
        surf = spad[pl.ds(8, RQ), mid]
        nsq = 1.0 + sx * sx + sy * sy
        rn = lax.rsqrt(nsq)
        pix[0] = surf
        pix[1] = -surf + sx * px + sy * py
        pix[2] = sx
        pix[3] = sy
        pix[4] = albedo[own, :] * rn
        pix[5] = mask[own, :].astype(f32) * rn
        pix[6] = rn * rn
        pix[7] = jnp.broadcast_to(px, (RQ, COLS))

        def unit(u, carry):
            r, c = unit_at(u)
            rs, cs = pl.ds(r, UNIT_ROWS), pl.ds(c, LANES)
            if it == 0:
                for j in range(NQ - 1):
                    ob_copy(j, u).wait_recv()
            sv, qv, sxv, syv, av = (pix[k, rs, cs] for k in range(5))
            low = None
            for l in range(NL):
                ls = pl.ds(l, 1)
                lxv, lyv, lzv, lev = (lights[k, ls, :] for k in range(4))
                dz = lzv - sv
                dist = dz * dz + c2[l, rs, cs]
                facing = (qv + lzv) - sxv * lxv - syv * lyv
                ri = lax.rsqrt(dist)
                r2 = ri * ri
                fall = lev * (r2 * ri)
                fac = fall * facing
                t = av * fac - obs_all[l, rs, cs].astype(f32)
                tt[l] = t
                ff[l] = fall
                fp[l] = fac
                gg[l] = dz * r2
                uu = t * t
                low = uu if low is None else jnp.minimum(low, uu)
            low = low * (0.5 * LOG2E)
            acc = None
            for l in range(NL):
                ls = pl.ds(l, 1)
                t = tt[l]
                p = jnp.exp2(low - (0.5 * LOG2E) * (t * t))
                w = p * t
                pull = w * ff[l]
                pf = w * fp[l]
                new = (p, pf, pf * gg[l], pull, pull * lights[0, ls, :], pull * lights[1, ls, :])
                acc = new if acc is None else tuple(a + b for a, b in zip(acc, new))
            ssum, A, D, PU, X, Y = acc
            pyv = pyb[0:UNIT_ROWS] + r.astype(f32) / TOTAL
            pxv = pix[7, rs, cs]
            scale = pix[5, rs, cs] / ssum
            alb = albedo[pl.ds(pl.multiple_of(base + r, UNIT_ROWS), UNIT_ROWS), cs]
            inv_n = pix[6, rs, cs]
            ga = scale * A
            ca = scale * alb
            tilt = ga * alb * inv_n
            ga_all[it, pl.ds(pl.multiple_of(base + r, UNIT_ROWS), UNIT_ROWS), cs] = ga
            gd[rs, cs] = ca * (3.0 * D - PU)
            gxpad[it, rs, pl.ds(pl.multiple_of(c + LANES, LANES), LANES)] = (
                ca * (pxv * PU - X) - tilt * sxv
            )
            gypad[it, pl.ds(pl.multiple_of(r + 8, 8), UNIT_ROWS), cs] = ca * (pyv * PU - Y) - tilt * syv
            return carry

        lax.fori_loop(0, nu // 2, unit, 0)
        gx = [
            remote(
                gxpad.at[it, :, pl.ds(COLS, LANES)], gxpad.at[it, :, lt],
                gx_send.at[it, 0], gx_recv.at[it, 0], right,
            ),
            remote(
                gxpad.at[it, :, pl.ds(LANES, LANES)], gxpad.at[it, :, rt],
                gx_send.at[it, 1], gx_recv.at[it, 1], left,
            ),
        ]
        for c in gx:
            c.start()
        lax.fori_loop(nu // 2, nu, unit, 0)
        gy = [
            remote(
                gypad.at[it, pl.ds(RQ, 8)], gypad.at[it, pl.ds(0, 8)],
                gy_send.at[it, 0], gy_recv.at[it, 0], (lax.rem(q + 1, NQ), s),
            ),
            remote(
                gypad.at[it, pl.ds(8, 8)], gypad.at[it, pl.ds(RQ + 8, 8)],
                gy_send.at[it, 1], gy_recv.at[it, 1], (lax.rem(q + NQ - 1, NQ), s),
            ),
        ]
        for c in gy:
            c.start()
        for c in gx + gy:
            c.wait()
        gxpad[it, :, lt] = gxpad[it, :, lt] * not_left
        gxpad[it, :, rt] = gxpad[it, :, rt] * not_right
        gypad[it, pl.ds(0, 8)] = gypad[it, pl.ds(0, 8)] * not_top
        gypad[it, pl.ds(RQ + 8, 8)] = gypad[it, pl.ds(RQ + 8, 8)] * not_bot
        lo, hi = shifted(gxpad.at[it])
        fd = gd[...] + 0.5 * (lo - hi) + 0.5 * (gypad[it, pl.ds(7, RQ)] - gypad[it, pl.ds(9, RQ)])
        fd_all[it, own, :] = fd
        ga = ga_all[it, own, :]

        def lanes(v):
            v = jnp.sum(v, axis=0, keepdims=True)
            return functools.reduce(lambda a, b: a + b, [v[:, k * LANES : (k + 1) * LANES] for k in range(ct)])

        total = jnp.concatenate([lanes(fd * fd), lanes(ga * ga)], axis=0)
        fs, fg = [], []
        for k in range(3):
            sums[it, k, pl.ds(slot[k], 1)] = total[None]
            cs = []
            for p in phases[k]:
                c = remote(
                    sums.at[it, k, slot[k]], sums.at[it, k, slot[k]], ar_send.at[it, k], ar_recv.at[it, k], p
                )
                c.start()
            if k == 0:
                if it == 0:
                    fs = [
                        remote(
                            fd_all.at[it, own, pl.ds(COLS - LANES, LANES)], fd_side.at[0],
                            fs_send.at[0], fs_recv.at[0], right,
                        ),
                        remote(
                            fd_all.at[it, own, pl.ds(0, LANES)], fd_side.at[1],
                            fs_send.at[1], fs_recv.at[1], left,
                        ),
                    ]
                for j, p in enumerate(mates):
                    for m, ref in enumerate((fd_all, ga_all)):
                        fg.append(
                            remote(
                                ref.at[it, own], ref.at[it, own], fd_send.at[it, j, m], fd_recv.at[it, j, m], p
                            )
                        )
                for c in fs + fg:
                    c.start()
            n = counts[k] - 1
            if n:
                whole = sums.at[it, k, pl.ds(0, n)]
                w = remote(whole, whole, ar_send.at[it, k], ar_recv.at[it, k], phases[k][0])
                w.wait_recv()
                w.wait_send()
            total = jnp.sum(sums[it, k], axis=0)
        for c in fs + fg:
            c.wait()
        means = jnp.sum(total, axis=1, keepdims=True) / (rows * float(TOTAL))
        inv = 1.0 / jnp.sqrt(means + epsilon)
        inv_d, inv_a = inv[0:1, 0:1], inv[1:2, 0:1]
        last = it == ITERS - 1
        new_depth = depth[...] - step_depth * jnp.tanh(fd_all[it] * inv_d)
        new_albedo = albedo[...] - step_albedo * jnp.tanh(ga_all[it] * inv_a)
        if last:
            depth_out[...] = new_depth
            albedo_out[...] = new_albedo
        else:
            depth[...] = new_depth
            albedo[...] = new_albedo
            fill_surface(depth)
            for m, (side, keep) in enumerate(((lt, not_left), (rt, not_right))):
                v = spad[pl.ds(8, RQ), side]
                spad[pl.ds(8, RQ), side] = keep * (v - step_depth * jnp.tanh(fd_side[m] * inv_d))

    def drain(u, carry):
        for j in range(NQ - 1):
            ob_copy(j, u).wait_send()
        return carry

    lax.fori_loop(0, nu, drain, 0)


def factors(n):
    return {128: (8, 8, 2)}.get(n, (n // 2, 1, 2) if n % 2 == 0 else (n, 1, 1))


def solution(mesh):
    NQ, NS = mesh.shape["light"], mesh.shape["strip"]

    def shards(depth, albedo, obs, table, mask):
        rows, cols = depth.shape
        nl = obs.shape[0]
        RQ = rows // NQ
        FACT = factors(NS)
        NL = NQ * nl
        nu = (RQ // UNIT_ROWS) * (cols // LANES)
        cfg = (NQ, NS, RQ, cols, cols * NS, FACT)
        wide = cols + 2 * LANES
        V, D = pltpu.VMEM, pltpu.SemaphoreType.DMA
        any_spec = pl.BlockSpec(memory_space=pl.ANY)
        vm = pl.BlockSpec(memory_space=pltpu.VMEM)
        out = jax.ShapeDtypeStruct((rows, cols), f32)
        return pl.pallas_call(
            functools.partial(kernel, cfg),
            out_shape=(out, out),
            in_specs=[any_spec] * 5,
            out_specs=(vm, vm),
            scratch_shapes=[
                V((rows, cols), f32), V((rows, cols), f32), V((rows, cols), jnp.int32), V((nl, 4), jnp.int32),
                V((NL, RQ, cols), jnp.bfloat16), V((NQ, nl, LANES), f32), V((4, NL, LANES), f32),
                V((cols // LANES, NL, LANES), f32), V((NL, RQ, cols), f32),
                V((RQ + 16, wide), f32), V((ITERS, RQ, wide), f32), V((ITERS, RQ + 16, cols), f32),
                V((RQ, cols), f32), V((8, RQ, cols), f32),
                V((NL, UNIT_ROWS, LANES), f32), V((NL, UNIT_ROWS, LANES), f32),
                V((NL, UNIT_ROWS, LANES), f32), V((NL, UNIT_ROWS, LANES), f32),
                V((ITERS, rows, cols), f32), V((ITERS, rows, cols), f32),
                V((2, RQ, LANES), f32), V((ITERS, 3, 8, 2, LANES), f32),
                D((5,)), D((NQ - 1, nu)), D((NQ - 1, nu)), D((NQ - 1,)), D((NQ - 1,)), D((2,)), D((2,)),
                D((ITERS, 2)), D((ITERS, 2)), D((ITERS, 2)), D((ITERS, 2)), D((2,)), D((2,)),
                D((ITERS, NQ - 1, 2)), D((ITERS, NQ - 1, 2)), D((ITERS, 3)), D((ITERS, 3)),
            ],
            compiler_params=pltpu.CompilerParams(
                collective_id=0, has_side_effects=True, vmem_limit_bytes=28 * 2**20
            ),
            cost_estimate=pl.CostEstimate(flops=10**8, bytes_accessed=3 * 2**20, transcendentals=10**6),
            name="steps",
        )(depth, albedo, obs, table, mask)

    in_specs = (
        P(None, "strip"),
        P(None, "strip"),
        P("light", None, "strip"),
        P("light", None),
        P(None, "strip"),
    )
    return jax.shard_map(
        shards, mesh=mesh, in_specs=in_specs, out_specs=(P(None, "strip"), P(None, "strip")), check_vma=False
    )
```

time: 1120 us -> 71.4 us (0.06)
  the two profiles are of different devices: /device:TPU:256 before, /device:TPU:1 now
where the time goes in v1:
time: 71.4 us; the launch traced here: 71.1 us
  Pallas kernels  64.3 us (90%)
  local copies, waits for them, and re-layouts  6.24 us (9%)
    pallas_call x1, Pallas kernels, shards(): pl.pallas_call(functools.partial(kernel, cfg), out_shape=(out, out), in_s...  64.3 us
    unnamed x11, local copies, waits for them, and re-layouts  6.24 us

profile of v1, /device:TPU:1, one launch (start us, length us, event | category | flops | bytes accessed | tf_op | source)
XLA Modules:
  0.0 71.1 jit_solution(8446848274945195935)
XLA Ops:
  0.6 0.8 %copy.7.table_hbm = s32[8,4]{1,0:T(8,128)S(1)} copy(s32[8,4]{0,1:T(4,128)} %param.8) | data formatting | bytes 256 | tf_op args[3]
  1.4 0.0 copy-start
  1.4 1.2 %copy-done = bf16[8,128,512]{2,1,0:T(8,128)(2,1)S(1)} copy-done((bf16[8,128,512]{2,1,0:T(8,128)(2,1)S(1)}, bf16[8,128,512]{2,1,0:T(8,128)(2,1)}, u32[]{:S(2)}) %copy-start) | copy-done | bytes 1048600
  2.6 0.0 copy-start.1
  2.6 0.9 %copy-done.1 = f32[128,512]{1,0:T(8,128)S(1)} copy-done((f32[128,512]{1,0:T(8,128)S(1)}, f32[128,512]{1,0:T(8,128)}, u32[]{:S(2)}) %copy-start.1) | copy-done | bytes 262168
  3.6 0.0 copy-start.2
  3.6 0.9 %copy-done.2 = f32[128,512]{1,0:T(8,128)S(1)} copy-done((f32[128,512]{1,0:T(8,128)S(1)}, f32[128,512]{1,0:T(8,128)}, u32[]{:S(2)}) %copy-start.2) | copy-done | bytes 262168
  4.5 0.0 copy-start.3
  4.5 0.9 %copy-done.3 = s32[128,512]{1,0:T(8,128)S(1)} copy-done((s32[128,512]{1,0:T(8,128)S(1)}, s32[128,512]{1,0:T(8,128)}, u32[]{:S(2)}) %copy-start.3) | copy-done | bytes 262168
  5.5 64.3 %steps.1 = (f32[128,512]{1,0:T(8,128)S(1)}, f32[128,512]{1,0:T(8,128)S(1)}) custom-call(f32[128,512]{1,0:T(8,128)S(1)} %copy-done.1, f32[128,512]{1,0:T(8,128)S(1)} %copy-done.2, bf16[8,128,512]{2,1,0:T(8,128)(2,1)S(1)} %copy-done, s32[8,4]{1,0:T(8,128)S(1)} %copy.7.table_hbm, s32[128,512]{1,0:T(8,128)S(1)} %copy-done.3), custom_call_target="tpu_custom_call" | custom-call | flops 100000000 | bytes 3145728 | tf_op jit(solution)/shard_map/steps/pallas_call | solution.py:387
  69.7 0.7 copy.10
  70.4 0.7 copy.11
Async XLA Ops:
  1.4 1.2 %copy-start = (bf16[8,128,512]{2,1,0:T(8,128)(2,1)S(1)}, bf16[8,128,512]{2,1,0:T(8,128)(2,1)}, u32[]{:S(2)}) copy-start(bf16[8,128,512]{2,1,0:T(8,128)(2,1)} %obs_hbm.1) | copy-start | bytes 3145732
  2.6 0.9 %copy-start.1 = (f32[128,512]{1,0:T(8,128)S(1)}, f32[128,512]{1,0:T(8,128)}, u32[]{:S(2)}) copy-start(f32[128,512]{1,0:T(8,128)} %depth_hbm.1) | copy-start | bytes 786436
  3.6 0.9 %copy-start.2 = (f32[128,512]{1,0:T(8,128)S(1)}, f32[128,512]{1,0:T(8,128)}, u32[]{:S(2)}) copy-start(f32[128,512]{1,0:T(8,128)} %albedo_hbm.1) | copy-start | bytes 786436
  4.5 0.9 %copy-start.3 = (s32[128,512]{1,0:T(8,128)S(1)}, s32[128,512]{1,0:T(8,128)}, u32[]{:S(2)}) copy-start(s32[128,512]{1,0:T(8,128)} %mask_hbm.1) | copy-start | bytes 786436

commit v2 on v1

--- a/solution.py
+++ b/solution.py
@@ -33,7 +33,7 @@
     depth, albedo, mask, table, obs_all, tables, lights,
     dx2, c2, spad, gxpad, gypad, gd, pix,
     tt, ff, fp, gg,
-    fd_all, ga_all, fd_side, sums,
+    fd_all, ga_all, fd_side, plane_sums, group_sums,
     in_sem, ob_send, ob_recv, tb_send, tb_recv, sd_send, sd_recv,
     gx_send, gx_recv, gy_send, gy_recv, fs_send, fs_recv, fd_send, fd_recv, ar_send, ar_recv,
 ):
@@ -51,18 +51,24 @@
     right = (q, lax.rem(s + 1, NS))
     left = (q, lax.rem(s + NS - 1, NS))
 
+    def ring(k, n):
+        return min(k, n - k)
+
+    plane = sorted(
+        [(a, b) for a in range(nz) for b in range(ny) if (a, b) != (0, 0)],
+        key=lambda o: -(ring(o[0], nz) + ring(o[1], ny)),
+    )
     phases = [
-        [(q, lax.rem(s + ny * nx * k, NS)) for k in range(1, nz)],
-        [(q, z * (ny * nx) + lax.rem(y * nx + xh + nx * k, ny * nx)) for k in range(1, ny)],
+        [(q, lax.rem(z + a, nz) * (ny * nx) + lax.rem(y + b, ny) * nx + xh) for a, b in plane],
         [
             (lax.rem(q + k, NQ), z * (ny * nx) + y * nx + lax.rem(xh + h, nx))
-            for h in range(nx)
-            for k in range(NQ)
+            for h in reversed(range(nx))
+            for k in (2, 3, 1, 0)
             if (h, k) != (0, 0)
         ],
     ]
-    slot = [z, y, q * nx + xh]
-    counts = [nz, ny, NQ * nx]
+    slot = [z * ny + y, q * nx + xh]
+    counts = [nz * ny, NQ * nx]
 
     base = pl.multiple_of(q * RQ, RQ)
     ins = [
@@ -84,8 +90,8 @@
     pl.semaphore_wait(barrier, len(partners))
 
     ins[3].wait()
-    tables[pl.ds(q, 1)] = jnp.zeros((1, nl, LANES), f32)
-    tables[pl.ds(q, 1), :, 0:4] = table[...].astype(f32)[None]
+    tables[pl.ds(q, 1)] = jnp.zeros((1, 4, LANES), f32)
+    tables[pl.ds(q, 1), :, 0:nl] = table[...].astype(f32)[None]
     tb = []
     for j, p in enumerate(mates):
         c = remote(tables.at[q], tables.at[q], tb_send.at[j], tb_recv.at[j], p)
@@ -131,11 +137,23 @@
 
     for c in tb:
         c.wait()
-    tab = tables[...].reshape(NL, LANES)
-    lx = tab[:, 0:1] / 500.0 - 1.0
-    ly = tab[:, 1:2] / 500.0 - 1.0
-    lz = 1.0 + tab[:, 2:3] / 1000.0
-    le = 0.5 + tab[:, 3:4] / 1000.0
+    diagonal = lax.broadcasted_iota(jnp.int32, (nl, LANES), 0) == lax.broadcasted_iota(
+        jnp.int32, (nl, LANES), 1
+    )
+
+    def component(k):
+        return jnp.concatenate(
+            [
+                jnp.sum(jnp.where(diagonal, tables[g, k : k + 1, :], 0.0), axis=1, keepdims=True)
+                for g in range(NQ)
+            ],
+            axis=0,
+        )
+
+    lx = component(0) / 500.0 - 1.0
+    ly = component(1) / 500.0 - 1.0
+    lz = 1.0 + component(2) / 1000.0
+    le = 0.5 + component(3) / 1000.0
     for k, v in enumerate((lx, ly, lz, le)):
         lights[k] = jnp.broadcast_to(v, (NL, LANES))
     col_i = lax.broadcasted_iota(jnp.int32, (1, COLS), 1) + s * COLS
@@ -189,6 +207,7 @@
         hi = pltpu.roll(x, width - 1, 1)[:, LANES : LANES + COLS]
         return lo, hi
 
+    sent = []
     for it in range(ITERS):
         lo, hi = shifted(spad)
         sx = 0.5 * (hi - lo)
@@ -301,14 +320,11 @@
 
         total = jnp.concatenate([lanes(fd * fd), lanes(ga * ga)], axis=0)
         fs, fg = [], []
-        for k in range(3):
-            sums[it, k, pl.ds(slot[k], 1)] = total[None]
-            cs = []
+        for k, sums in enumerate((plane_sums, group_sums)):
+            sums[it, pl.ds(slot[k], 1)] = total[None]
+            mine = sums.at[it, slot[k]]
             for p in phases[k]:
-                c = remote(
-                    sums.at[it, k, slot[k]], sums.at[it, k, slot[k]], ar_send.at[it, k], ar_recv.at[it, k], p
-                )
-                c.start()
+                remote(mine, mine, ar_send.at[it, k], ar_recv.at[it, k], p).start()
             if k == 0:
                 if it == 0:
                     fs = [
@@ -332,11 +348,11 @@
                     c.start()
             n = counts[k] - 1
             if n:
-                whole = sums.at[it, k, pl.ds(0, n)]
+                whole = sums.at[it, pl.ds(0, n)]
                 w = remote(whole, whole, ar_send.at[it, k], ar_recv.at[it, k], phases[k][0])
                 w.wait_recv()
-                w.wait_send()
-            total = jnp.sum(sums[it, k], axis=0)
+                sent.append(w)
+            total = jnp.sum(sums[it], axis=0)
         for c in fs + fg:
             c.wait()
         means = jnp.sum(total, axis=1, keepdims=True) / (rows * float(TOTAL))
@@ -362,6 +378,8 @@
         return carry
 
     lax.fori_loop(0, nu, drain, 0)
+    for w in sent:
+        w.wait_send()
 
 
 def factors(n):
@@ -390,25 +408,26 @@
             in_specs=[any_spec] * 5,
             out_specs=(vm, vm),
             scratch_shapes=[
-                V((rows, cols), f32), V((rows, cols), f32), V((rows, cols), jnp.int32), V((nl, 4), jnp.int32),
-                V((NL, RQ, cols), jnp.bfloat16), V((NQ, nl, LANES), f32), V((4, NL, LANES), f32),
+                V((rows, cols), f32), V((rows, cols), f32), V((rows, cols), jnp.int32), V((4, nl), jnp.int32),
+                V((NL, RQ, cols), jnp.bfloat16), V((NQ, 4, LANES), f32), V((4, NL, LANES), f32),
                 V((cols // LANES, NL, LANES), f32), V((NL, RQ, cols), f32),
                 V((RQ + 16, wide), f32), V((ITERS, RQ, wide), f32), V((ITERS, RQ + 16, cols), f32),
                 V((RQ, cols), f32), V((8, RQ, cols), f32),
                 V((NL, UNIT_ROWS, LANES), f32), V((NL, UNIT_ROWS, LANES), f32),
                 V((NL, UNIT_ROWS, LANES), f32), V((NL, UNIT_ROWS, LANES), f32),
                 V((ITERS, rows, cols), f32), V((ITERS, rows, cols), f32),
-                V((2, RQ, LANES), f32), V((ITERS, 3, 8, 2, LANES), f32),
+                V((2, RQ, LANES), f32),
+                V((ITERS, FACT[0] * FACT[1], 2, LANES), f32), V((ITERS, NQ * FACT[2], 2, LANES), f32),
                 D((5,)), D((NQ - 1, nu)), D((NQ - 1, nu)), D((NQ - 1,)), D((NQ - 1,)), D((2,)), D((2,)),
                 D((ITERS, 2)), D((ITERS, 2)), D((ITERS, 2)), D((ITERS, 2)), D((2,)), D((2,)),
-                D((ITERS, NQ - 1, 2)), D((ITERS, NQ - 1, 2)), D((ITERS, 3)), D((ITERS, 3)),
+                D((ITERS, NQ - 1, 2)), D((ITERS, NQ - 1, 2)), D((ITERS, 2)), D((ITERS, 2)),
             ],
             compiler_params=pltpu.CompilerParams(
-                collective_id=0, has_side_effects=True, vmem_limit_bytes=28 * 2**20
+                collective_id=0, has_side_effects=True, vmem_limit_bytes=56 * 2**20
             ),
             cost_estimate=pl.CostEstimate(flops=10**8, bytes_accessed=3 * 2**20, transcendentals=10**6),
             name="steps",
-        )(depth, albedo, obs, table, mask)
+        )(depth, albedo, obs, table.T, mask)
 
     in_specs = (
         P(None, "strip"),

time: 71.4 us -> 65.8 us (0.922)
  local copies, waits for them, and re-layouts: 6.24 us -> 2.42 us
  Pallas kernels: 64.3 us -> 62.6 us
    unnamed x11 -> x4, local copies, waits for them, and re-layouts: 6.24 us -> 2.42 us
    pallas_call x1, Pallas kernels: 64.3 us -> 62.6 us  [shards(): pl.pallas_call(functools.partial(kernel, cfg), out_shape=(out, out), in_s...]
where the time goes in v2:
time: 65.8 us; the launch traced here: 65.6 us
  Pallas kernels  62.6 us (95%)
  local copies, waits for them, and re-layouts  2.42 us (4%)
    pallas_call x1, Pallas kernels, shards(): pl.pallas_call(functools.partial(kernel, cfg), out_shape=(out, out), in_s...  62.6 us
    unnamed x4, local copies, waits for them, and re-layouts  2.42 us

profile of v2, /device:TPU:1, one launch (start us, length us, event | category | flops | bytes accessed | tf_op | source)
XLA Modules:
  0.0 65.6 jit_solution(5305529512774283452)
XLA Ops:
  0.6 62.6 %steps.1 = (f32[128,512]{1,0:T(8,128)}, f32[128,512]{1,0:T(8,128)}) custom-call(f32[128,512]{1,0:T(8,128)} %depth_hbm.1, f32[128,512]{1,0:T(8,128)} %albedo_hbm.1, bf16[8,128,512]{2,1,0:T(8,128)(2,1)} %obs_hbm.1, s32[4,8]{1,0:T(4,128)} %bitcast.1, s32[128,512]{1,0:T(8,128)} %mask_hbm.1), custom_call_target="tpu_custom_call" | custom-call | flops 100000000 | bytes 3145728 | tf_op jit(solution)/shard_map/steps/pallas_call | solution.py:405
  63.2 0.0 copy-start
  63.2 1.7 %copy.9 = f32[128,512]{1,0:T(8,128)} copy(f32[128,512]{1,0:T(8,128)} %get-tuple-element.4) | data formatting | bytes 524288
  64.9 0.0 copy-done
  64.9 0.7 %copy.10 = f32[128,512]{1,0:T(8,128)} copy(f32[128,512]{1,0:T(8,128)S(1)} %copy-done) | data formatting | bytes 524288
Async XLA Ops:
  63.2 1.7 %copy-start = (f32[128,512]{1,0:T(8,128)S(1)}, f32[128,512]{1,0:T(8,128)}, u32[]{:S(2)}) copy-start(f32[128,512]{1,0:T(8,128)} %get-tuple-element.5) | copy-start | bytes 786436

commit v3 on v2

v3 whole, which is shorter than its diff:
```python
import functools

import jax
import jax.numpy as jnp
from jax import lax
from jax.experimental import pallas as pl
from jax.experimental.pallas import tpu as pltpu
from jax.sharding import PartitionSpec as P

MESH = pl.DeviceIdType.MESH
ITERS = 2
step_depth = 0.1
step_albedo = 0.2
epsilon = 1e-06
HALF_LOG2E = 0.5 * 1.4426950408889634

UNIT = 16
LANES = 128
f32 = jnp.float32


def remote(src, dst, send, recv, device):
    return pltpu.make_async_remote_copy(
        src_ref=src, dst_ref=dst, send_sem=send, recv_sem=recv, device_id=device, device_id_type=MESH
    )


def kernel(
    cfg,
    depth_hbm, albedo_hbm, obs_hbm, table_hbm, mask_hbm,
    depth_out, albedo_out,
    depth, albedo, mask, table, obs_own, obs_all, tables, lights,
    staged, dx2, c2, spad, alb_own, gx, gypad, gd, pix,
    tt, ff, fp, gg,
    edge_obs, halo_obs, halo_loop, pack_out, pack_in, halo,
    fd_all, ga_all, near_sums, far_sums,
    in_sem, st_sem, ob_send, ob_recv, tb_send, tb_recv, eo_send, eo_recv, lo_send, lo_recv,
    pk_send, pk_recv, fd_send, fd_recv, ar_send, ar_recv,
):
    NQ, NS, COLS, TOTAL, FACT = cfg
    nl = obs_hbm.shape[0]
    rows = depth_hbm.shape[0]
    nu = rows // UNIT
    NL = NQ * nl
    q = lax.axis_index("light")
    s = lax.axis_index("strip")
    nz, ny, nx = FACT
    z, y, xh = s // (ny * nx), lax.rem(s, ny * nx) // nx, lax.rem(s, nx)
    up, down = lax.rem(s + 1, NS), lax.rem(s + NS - 1, NS)
    others = [lax.rem(q + k, NQ) for k in (2, 3, 1)]
    across, mate = (q ^ 2, s), (q ^ 1, s)
    right = (lax.rem(q + 1, NQ), jnp.where(q == NQ - 1, up, s))
    left = (lax.rem(q + NQ - 1, NQ), jnp.where(q == 0, down, s))

    def ring(k, n):
        return min(k, n - k)

    plane = sorted(
        [(a, b) for a in range(nz) for b in range(ny) if (a, b) != (0, 0)],
        key=lambda o: -(ring(o[0], nz) + ring(o[1], ny)),
    )
    phases = [
        [
            (lax.rem(q + k, NQ), z * (ny * nx) + y * nx + lax.rem(xh + h, nx))
            for h in reversed(range(nx))
            for k in (2, 3, 1, 0)
            if (h, k) != (0, 0)
        ],
        [(q, lax.rem(z + a, nz) * (ny * nx) + lax.rem(y + b, ny) * nx + xh) for a, b in plane],
    ]
    slot = [q * nx + xh, z * ny + y]
    counts = [NQ * nx, nz * ny]

    base = pl.multiple_of(q * LANES, LANES)
    own = pl.ds(base, LANES)
    ins = [
        pltpu.make_async_copy(table_hbm, table, in_sem.at[0]),
        pltpu.make_async_copy(depth_hbm, depth, in_sem.at[1]),
        pltpu.make_async_copy(albedo_hbm, albedo, in_sem.at[2]),
        pltpu.make_async_copy(mask_hbm, mask, in_sem.at[3]),
        pltpu.make_async_copy(obs_hbm, obs_own, in_sem.at[4]),
    ]
    mine = pl.ds(pl.multiple_of(q * nl, nl), nl)

    def block(t, u):
        r = pl.ds(pl.multiple_of(u * UNIT, UNIT), UNIT)
        return obs_hbm.at[:, r, pl.ds(pl.multiple_of(t * LANES, LANES), LANES)]

    def stage(u, carry):
        for j, t in enumerate(others):
            pltpu.make_async_copy(block(t, u), staged.at[j, u], st_sem.at[j]).start()
        return carry

    def stage_own(u, carry):
        pltpu.make_async_copy(block(q, u), obs_all.at[u, mine], st_sem.at[NQ - 1]).start()
        return carry

    ins[0].start()
    lax.fori_loop(0, nu, stage, 0)
    lax.fori_loop(0, nu, stage_own, 0)
    for c in ins[1:]:
        c.start()

    barrier = pltpu.get_barrier_semaphore()
    beside = [(lax.rem(q + k, NQ), t) for k in range(NQ) for t in (up, down)]
    partners = phases[0] + beside + phases[1]
    for p in partners:
        pl.semaphore_signal(barrier, inc=1, device_id=p, device_id_type=MESH)

    def ob_copy(j, u):
        t = others[j]
        return remote(
            staged.at[j, u], obs_all.at[u, mine], ob_send.at[j, u], ob_recv.at[j, u], (t, s)
        )

    def send_obs(u, carry):
        for j in range(NQ - 1):
            ob_copy(j, u).start()
        return carry

    eye = lax.broadcasted_iota(jnp.int32, (rows, LANES), 0) == lax.broadcasted_iota(jnp.int32, (rows, LANES), 1)
    lane = lax.broadcasted_iota(jnp.int32, (rows, LANES), 1)
    lane1 = lax.broadcasted_iota(jnp.int32, (1, LANES), 1)

    def to_lanes(v, c):
        return jnp.sum(jnp.where(eye, jnp.broadcast_to(v[:, c : c + 1], (rows, LANES)), 0.0), axis=0, keepdims=True)

    def to_rows(v):
        return jnp.sum(jnp.where(eye, jnp.broadcast_to(v, (rows, LANES)), 0.0), axis=1, keepdims=True)

    def pack_edges(it, fields):
        k = 0
        for v, far in fields:
            pack_out[it, 0, k : k + 1, :] = to_lanes(v, LANES - 1)
            pack_out[it, 1, k : k + 1, :] = to_lanes(v, 0)
            k += 1
            if far:
                pack_out[it, 0, k : k + 1, :] = to_lanes(v, LANES - 2)
                pack_out[it, 1, k : k + 1, :] = to_lanes(v, 1)
                k += 1

    def send_edges(it):
        out = [
            remote(pack_out.at[it, 0], pack_in.at[it, 0], pk_send.at[it, 0], pk_recv.at[it, 0], right),
            remote(pack_out.at[it, 1], pack_in.at[it, 1], pk_send.at[it, 1], pk_recv.at[it, 1], left),
        ]
        for c in out:
            c.start()
        return out

    for k in (1, 2, 3):
        ins[k].wait()
    center = pl.ds(8, rows)
    spad[...] = jnp.zeros_like(spad)
    gypad[...] = jnp.zeros_like(gypad)
    pack_out[...] = jnp.zeros_like(pack_out)
    spad[center, :] = depth[:, own]
    alb_own[...] = albedo[:, own]
    pack_edges(
        0, ((depth[:, own], True), (alb_own[...], False), (mask[:, own].astype(f32), False))
    )

    ins[0].wait()
    tables[pl.ds(q, 1)] = jnp.zeros((1, 4, LANES), f32)
    tables[pl.ds(q, 1), :, 0:nl] = table[...].astype(f32)[None]
    ins[4].wait()
    e_row = lax.broadcasted_iota(jnp.int32, (2 * NQ, COLS), 0)
    e_col = lax.broadcasted_iota(jnp.int32, (2 * NQ, COLS), 1)
    wanted = lax.rem((e_row // 2) * LANES + jnp.where(lax.rem(e_row, 2) == 0, COLS - 1, LANES), COLS)
    pick = jnp.where(e_col == wanted, 1.0, 0.0).astype(jnp.bfloat16)
    for l in range(nl):
        got = lax.dot_general(
            pick, obs_own[l], (((1,), (1,)), ((), ())), preferred_element_type=f32
        )
        for e in range(2 * NQ):
            edge_obs[e, l : l + 1, :] = got[e : e + 1]
    pl.semaphore_wait(barrier, len(partners))
    tb = [
        remote(tables.at[q], tables.at[q], tb_send.at[j], tb_recv.at[j], (t, s)) for j, t in enumerate(others)
    ]
    for c in tb:
        c.start()

    pk = send_edges(0)
    eo = []
    for j, t in enumerate(others):
        for side in range(2):
            strip = jnp.where(t == 0, up, s) if side == 0 else jnp.where(t == NQ - 1, down, s)
            eo.append(
                remote(
                    edge_obs.at[2 * t + side], halo_obs.at[side, mine],
                    eo_send.at[j, side], eo_recv.at[j, side], (t, strip),
                )
            )
    lo = [
        remote(edge_obs.at[0], halo_loop.at[0], lo_send.at[0], lo_recv.at[0], (q, up)),
        remote(edge_obs.at[2 * NQ - 1], halo_loop.at[1], lo_send.at[1], lo_recv.at[1], (q, down)),
    ]
    for c in eo + lo:
        c.start()

    for j in range(NQ - 1):
        pltpu.make_async_copy(staged.at[j], staged.at[j], st_sem.at[j]).wait()
    lax.fori_loop(0, nu, send_obs, 0)

    for c in tb:
        c.wait()
    diagonal = lax.broadcasted_iota(jnp.int32, (nl, LANES), 0) == lax.broadcasted_iota(jnp.int32, (nl, LANES), 1)

    def component(k):
        return jnp.concatenate(
            [
                jnp.sum(jnp.where(diagonal, tables[g, k : k + 1, :], 0.0), axis=1, keepdims=True)
                for g in range(NQ)
            ],
            axis=0,
        )

    lx = component(0) / 500.0 - 1.0
    ly = component(1) / 500.0 - 1.0
    lz = 1.0 + component(2) / 1000.0
    le = 0.5 + component(3) / 1000.0
    for k, v in enumerate((lx, ly, lz, le)):
        lights[k] = jnp.broadcast_to(v, (NL, LANES))

    def coord_x(columns):
        return (columns.astype(f32) + 0.5) / TOTAL - 0.5

    def coord_y(index):
        return (index.astype(f32) + 0.5 - rows / 2.0) / TOTAL

    first = s * COLS + q * LANES
    px = coord_x(lane1 + first)
    py = coord_y(lax.broadcasted_iota(jnp.int32, (rows, LANES), 0))
    py_lane = coord_y(lane1)
    d = lx - px
    dx2[...] = d * d

    def make_c2(l, carry):
        dy = lights[1, pl.ds(l, 1), :] - py
        c2[l] = dy * dy + dx2[pl.ds(l, 1), :]
        return carry

    lax.fori_loop(0, NL, make_c2, 0)

    not_left = jnp.where((s == 0) & (q == 0), 0.0, 1.0).astype(f32)
    not_right = jnp.where((s == NS - 1) & (q == NQ - 1), 0.0, 1.0).astype(f32)
    keep = (not_left, not_right)

    for c in pk + eo + lo:
        c.wait()
    for side in range(2):
        inner = edge_obs[2 * q + side]
        at_end = (q == 0) if side == 0 else (q == NQ - 1)
        halo_obs[side, mine, :] = jnp.where(at_end, halo_loop[side], inner)
        v = pack_in[0, side]
        halo[side, 0:2, :] = v[0:2] * keep[side]
        halo[side, 2:4, :] = v[2:4]
    pltpu.make_async_copy(obs_all.at[:, mine], obs_all.at[:, mine], st_sem.at[NQ - 1]).wait()

    def widen(v, lo_col, hi_col):
        lo_v = jnp.where(lane == 0, lo_col, pltpu.roll(v, 1, 1))
        hi_v = jnp.where(lane == LANES - 1, hi_col, pltpu.roll(v, LANES - 1, 1))
        return lo_v, hi_v

    def side_gradient(side):
        near, far, alb, val = (halo[side, k : k + 1, :] for k in range(4))
        surf = spad[center, :]
        inside = to_lanes(surf, 0 if side == 0 else LANES - 1)
        sx = 0.5 * (inside - far) if side == 0 else 0.5 * (far - inside)
        below = jnp.where(lane1 == LANES - 1, 0.0, pltpu.roll(near, LANES - 1, 1))
        above = jnp.where(lane1 == 0, 0.0, pltpu.roll(near, 1, 1))
        sy = 0.5 * (below - above)
        nsq = 1.0 + sx * sx + sy * sy
        rn = lax.rsqrt(nsq)
        pxs = coord_x(jnp.full((1, LANES), first, jnp.int32) + (-1 if side == 0 else LANES))
        lxs, lys, lzs, les = (lights[k] for k in range(4))
        dx, dy, dz = lxs - pxs, lys - py_lane, lzs - near
        dist = dx * dx + dy * dy + dz * dz
        facing = dz - sx * dx - sy * dy
        ri = lax.rsqrt(dist)
        fall = les * (ri * ri * ri)
        t = (alb * rn) * (fall * facing) - halo_obs[side]
        uu = t * t
        p = jnp.exp2(HALF_LOG2E * (jnp.min(uu, axis=0, keepdims=True) - uu))
        pull = p * t * fall
        total = jnp.sum(p, axis=0, keepdims=True)
        inner = jnp.sum(pull * dx, axis=0, keepdims=True) + (sx * rn * rn) * jnp.sum(
            pull * facing, axis=0, keepdims=True
        )
        return to_rows(-(keep[side] * val * rn * alb / total) * inner)

    sent, gathered = [], []
    for it in range(ITERS):
        last = it == ITERS - 1
        surf = spad[center, :]
        lo_v, hi_v = widen(surf, to_rows(halo[0, 0:1, :]), to_rows(halo[1, 0:1, :]))
        sx = 0.5 * (hi_v - lo_v)
        sy = 0.5 * (spad[pl.ds(9, rows), :] - spad[pl.ds(7, rows), :])
        nsq = 1.0 + sx * sx + sy * sy
        rn = lax.rsqrt(nsq)
        pix[0] = surf
        pix[1] = -surf + sx * px + sy * py
        pix[2] = sx
        pix[3] = sy
        pix[4] = alb_own[...] * rn
        pix[5] = mask[:, own].astype(f32) * rn
        pix[6] = rn * rn
        gx_lo, gx_hi = side_gradient(0), side_gradient(1)

        def unit(u, carry):
            rs = pl.ds(pl.multiple_of(u * UNIT, UNIT), UNIT)
            if it == 0:
                for j in range(NQ - 1):
                    ob_copy(j, u).wait_recv()
            sv, qv, sxv, syv, av = (pix[k, rs, :] for k in range(5))
            low = None
            for l in range(NL):
                ls = pl.ds(l, 1)
                lxv, lyv, lzv, lev = (lights[k, ls, :] for k in range(4))
                dz = lzv - sv
                dist = dz * dz + c2[l, rs, :]
                facing = (qv + lzv) - sxv * lxv - syv * lyv
                ri = lax.rsqrt(dist)
                r2 = ri * ri
                fall = lev * (r2 * ri)
                fac = fall * facing
                t = av * fac - obs_all[u, l].astype(f32)
                tt[l] = t
                ff[l] = fall
                fp[l] = fac
                gg[l] = dz * r2
                uu = t * t
                low = uu if low is None else jnp.minimum(low, uu)
            low = low * HALF_LOG2E
            acc = None
            for l in range(NL):
                ls = pl.ds(l, 1)
                t = tt[l]
                p = jnp.exp2(low - HALF_LOG2E * (t * t))
                w = p * t
                pull = w * ff[l]
                pf = w * fp[l]
                new = (p, pf, pf * gg[l], pull, pull * lights[0, ls, :], pull * lights[1, ls, :])
                acc = new if acc is None else tuple(a + b for a, b in zip(acc, new))
            ssum, A, D, PU, X, Y = acc
            pyv = py[0:UNIT] + lax.convert_element_type(u * UNIT, f32) / TOTAL
            scale = pix[5, rs, :] / ssum
            alb = alb_own[rs, :]
            ga = scale * A
            ca = scale * alb
            tilt = ga * alb * pix[6, rs, :]
            ga_all[it, rs, own] = ga
            gd[rs, :] = ca * (3.0 * D - PU)
            gx[rs, :] = ca * (px * PU - X) - tilt * sxv
            gypad[pl.ds(pl.multiple_of(u * UNIT + 8, 8), UNIT), :] = ca * (pyv * PU - Y) - tilt * syv
            return carry

        lax.fori_loop(0, nu, unit, 0)
        lo_v, hi_v = widen(gx[...], gx_lo, gx_hi)
        fd = gd[...] + 0.5 * (lo_v - hi_v) + 0.5 * (gypad[pl.ds(7, rows), :] - gypad[pl.ds(9, rows), :])
        ga = ga_all[it, :, own]
        total = jnp.concatenate(
            [jnp.sum(fd * fd, axis=0, keepdims=True), jnp.sum(ga * ga, axis=0, keepdims=True)], axis=0
        )
        for k, sums in enumerate((near_sums, far_sums)):
            sums[it, pl.ds(slot[k], 1)] = total[None]
            part = sums.at[it, slot[k]]
            for p in phases[k]:
                remote(part, part, ar_send.at[it, k], ar_recv.at[it, k], p).start()
            if k == 0:
                fd_all[it, :, own] = fd
                theirs = pl.ds(pl.multiple_of((q ^ 2) * LANES, LANES), LANES)

                def moves(n, cols, device):
                    return [
                        remote(
                            ref.at[it, :, cols], ref.at[it, :, cols], fd_send.at[it, n, m], fd_recv.at[it, n, m], device
                        )
                        for m, ref in enumerate((fd_all, ga_all))
                    ]

                over, to_mate, onward = moves(0, own, across), moves(1, own, mate), moves(2, theirs, mate)
                if not last:
                    pack_edges(1, ((fd, True), (ga, False)))
                    pk = send_edges(1)
                for c in over + to_mate:
                    c.start()
            else:
                for c in over:
                    c.wait()
                for c in onward:
                    c.start()
                if last:
                    for c in gathered:
                        c.wait()
                    depth[...] = depth[...] - step_depth * jnp.tanh(fd_all[0] * inv_d)
                    albedo[...] = albedo[...] - step_albedo * jnp.tanh(ga_all[0] * inv_a)
            whole = sums.at[it, pl.ds(0, counts[k] - 1)]
            w = remote(whole, whole, ar_send.at[it, k], ar_recv.at[it, k], phases[k][0])
            w.wait_recv()
            sent.append(w)
            total = jnp.sum(sums[it], axis=0)
        means = jnp.sum(total, axis=1, keepdims=True) / (rows * float(TOTAL))
        inv = 1.0 / jnp.sqrt(means + epsilon)
        inv_d, inv_a = inv[0:1, 0:1], inv[1:2, 0:1]
        if last:
            for c in to_mate + onward:
                c.wait()
            depth_out[...] = depth[...] - step_depth * jnp.tanh(fd_all[it] * inv_d)
            albedo_out[...] = albedo[...] - step_albedo * jnp.tanh(ga_all[it] * inv_a)
        else:
            gathered = to_mate + onward
            spad[center, :] = spad[center, :] - step_depth * jnp.tanh(fd_all[it, :, own] * inv_d)
            alb_own[...] = alb_own[...] - step_albedo * jnp.tanh(ga_all[it, :, own] * inv_a)
            for c in pk:
                c.wait()
            for side in range(2):
                v = pack_in[1, side]
                halo[side, 0:2, :] = keep[side] * (halo[side, 0:2, :] - step_depth * jnp.tanh(v[0:2] * inv_d))
                halo[side, 2:3, :] = halo[side, 2:3, :] - step_albedo * jnp.tanh(v[2:3] * inv_a)

    def drain(u, carry):
        for j in range(NQ - 1):
            ob_copy(j, u).wait_send()
        return carry

    lax.fori_loop(0, nu, drain, 0)
    for w in sent:
        w.wait_send()


def factors(n):
    return {128: (8, 8, 2)}[n]


def solution(mesh):
    NQ, NS = mesh.shape["light"], mesh.shape["strip"]

    def shards(depth, albedo, obs, table, mask):
        rows, cols = depth.shape
        nl = obs.shape[0]
        FACT = factors(NS)
        NL = NQ * nl
        nu = rows // UNIT
        cfg = (NQ, NS, cols, cols * NS, FACT)
        V, D = pltpu.VMEM, pltpu.SemaphoreType.DMA
        any_spec = pl.BlockSpec(memory_space=pl.ANY)
        vm = pl.BlockSpec(memory_space=pltpu.VMEM)
        out = jax.ShapeDtypeStruct((rows, cols), f32)
        return pl.pallas_call(
            functools.partial(kernel, cfg),
            out_shape=(out, out),
            in_specs=[any_spec] * 5,
            out_specs=(vm, vm),
            scratch_shapes=[
                V((rows, cols), f32), V((rows, cols), f32), V((rows, cols), jnp.int32), V((4, nl), jnp.int32),
                V((nl, rows, cols), jnp.bfloat16), V((nu, NL, UNIT, LANES), jnp.bfloat16),
                V((NQ, 4, LANES), f32), V((4, NL, LANES), f32),
                V((NQ - 1, nu, nl, UNIT, LANES), jnp.bfloat16),
                V((NL, LANES), f32), V((NL, rows, LANES), f32), V((rows + 16, LANES), f32), V((rows, LANES), f32),
                V((rows, LANES), f32), V((rows + 16, LANES), f32), V((rows, LANES), f32), V((7, rows, LANES), f32),
                V((NL, UNIT, LANES), f32), V((NL, UNIT, LANES), f32),
                V((NL, UNIT, LANES), f32), V((NL, UNIT, LANES), f32),
                V((2 * NQ, nl, LANES), f32), V((2, NL, LANES), f32), V((2, nl, LANES), f32),
                V((ITERS, 2, 8, LANES), f32), V((ITERS, 2, 8, LANES), f32), V((2, 8, LANES), f32),
                V((ITERS, rows, cols), f32), V((ITERS, rows, cols), f32),
                V((ITERS, NQ * FACT[2], 2, LANES), f32), V((ITERS, FACT[0] * FACT[1], 2, LANES), f32),
                D((5,)), D((NQ,)), D((NQ - 1, nu)), D((NQ - 1, nu)), D((NQ - 1,)), D((NQ - 1,)),
                D((NQ - 1, 2)), D((NQ - 1, 2)), D((2,)), D((2,)),
                D((ITERS, 2)), D((ITERS, 2)), D((ITERS, 3, 2)), D((ITERS, 3, 2)), D((ITERS, 2)), D((ITERS, 2)),
            ],
            compiler_params=pltpu.CompilerParams(
                collective_id=0, has_side_effects=True, vmem_limit_bytes=56 * 2**20
            ),
            cost_estimate=pl.CostEstimate(flops=10**8, bytes_accessed=3 * 2**20, transcendentals=10**6),
            name="steps",
        )(depth, albedo, obs, table.T, mask)

    in_specs = (
        P(None, "strip"),
        P(None, "strip"),
        P("light", None, "strip"),
        P("light", None),
        P(None, "strip"),
    )
    return jax.shard_map(
        shards, mesh=mesh, in_specs=in_specs, out_specs=(P(None, "strip"), P(None, "strip")), check_vma=False
    )
```

time: 65.8 us -> 59 us (0.90)
  Pallas kernels: 62.6 us -> 55.8 us
    pallas_call x1, Pallas kernels: 62.6 us -> 55.8 us  [shards(): pl.pallas_call(functools.partial(kernel, cfg), out_shape=(out, out), in_s...]
where the time goes in v3:
time: 59 us; the launch traced here: 58.9 us
  Pallas kernels  55.8 us (95%)
  local copies, waits for them, and re-layouts  2.42 us (4%)
  between operations  0.65 us (1%)
    pallas_call x1, Pallas kernels, shards(): pl.pallas_call(functools.partial(kernel, cfg), out_shape=(out, out), in_s...  55.8 us
    unnamed x4, local copies, waits for them, and re-layouts  2.42 us

profile of v3, /device:TPU:1, one launch (start us, length us, event | category | flops | bytes accessed | tf_op | source)
XLA Modules:
  0.0 58.9 jit_solution(12361397798154021582)
XLA Ops:
  0.6 55.8 %steps.1 = (f32[128,512]{1,0:T(8,128)}, f32[128,512]{1,0:T(8,128)}) custom-call(f32[128,512]{1,0:T(8,128)} %depth_hbm.1, f32[128,512]{1,0:T(8,128)} %albedo_hbm.1, bf16[8,128,512]{2,1,0:T(8,128)(2,1)} %obs_hbm.1, s32[4,8]{1,0:T(4,128)} %bitcast.1, s32[128,512]{1,0:T(8,128)} %mask_hbm.1), custom_call_target="tpu_custom_call" | custom-call | flops 100000000 | bytes 3145728 | tf_op jit(solution)/shard_map/steps/pallas_call | solution.py:451
  56.4 0.0 copy-start
  56.4 1.7 %copy.9 = f32[128,512]{1,0:T(8,128)} copy(f32[128,512]{1,0:T(8,128)} %get-tuple-element.4) | data formatting | bytes 524288
  58.1 0.0 copy-done
  58.1 0.7 %copy.10 = f32[128,512]{1,0:T(8,128)} copy(f32[128,512]{1,0:T(8,128)S(1)} %copy-done) | data formatting | bytes 524288
Async XLA Ops:
  56.4 1.7 %copy-start = (f32[128,512]{1,0:T(8,128)S(1)}, f32[128,512]{1,0:T(8,128)}, u32[]{:S(2)}) copy-start(f32[128,512]{1,0:T(8,128)} %get-tuple-element.5) | copy-start | bytes 786436

commit v4 on v3

--- a/solution.py
+++ b/solution.py
@@ -13,8 +13,10 @@
 step_albedo = 0.2
 epsilon = 1e-06
 HALF_LOG2E = 0.5 * 1.4426950408889634
+ROOT = HALF_LOG2E ** 0.5
 
 UNIT = 16
+AHEAD = 3
 LANES = 128
 f32 = jnp.float32
 
@@ -27,10 +29,10 @@
 
 def kernel(
     cfg,
-    depth_hbm, albedo_hbm, obs_hbm, table_hbm, mask_hbm,
+    depth_hbm, albedo_hbm, obs_hbm, table_ref, mask_hbm,
     depth_out, albedo_out,
-    depth, albedo, mask, table, obs_own, obs_all, tables, lights,
-    staged, dx2, c2, spad, alb_own, gx, gypad, gd, pix,
+    depth, albedo, mask, obs_own, obs_all, tables, lights,
+    staged, dx1, dy1, obs_f, c2, spad, alb_own, gx, gypad, gd, pix,
     tt, ff, fp, gg,
     edge_obs, halo_obs, halo_loop, pack_out, pack_in, halo,
     fd_all, ga_all, near_sums, far_sums,
@@ -71,41 +73,40 @@
     slot = [q * nx + xh, z * ny + y]
     counts = [NQ * nx, nz * ny]
 
-    base = pl.multiple_of(q * LANES, LANES)
-    own = pl.ds(base, LANES)
-    ins = [
-        pltpu.make_async_copy(table_hbm, table, in_sem.at[0]),
-        pltpu.make_async_copy(depth_hbm, depth, in_sem.at[1]),
-        pltpu.make_async_copy(albedo_hbm, albedo, in_sem.at[2]),
-        pltpu.make_async_copy(mask_hbm, mask, in_sem.at[3]),
-        pltpu.make_async_copy(obs_hbm, obs_own, in_sem.at[4]),
-    ]
-    mine = pl.ds(pl.multiple_of(q * nl, nl), nl)
-
-    def block(t, u):
-        r = pl.ds(pl.multiple_of(u * UNIT, UNIT), UNIT)
-        return obs_hbm.at[:, r, pl.ds(pl.multiple_of(t * LANES, LANES), LANES)]
-
-    def stage(u, carry):
-        for j, t in enumerate(others):
-            pltpu.make_async_copy(block(t, u), staged.at[j, u], st_sem.at[j]).start()
-        return carry
-
-    def stage_own(u, carry):
-        pltpu.make_async_copy(block(q, u), obs_all.at[u, mine], st_sem.at[NQ - 1]).start()
-        return carry
-
-    ins[0].start()
-    lax.fori_loop(0, nu, stage, 0)
-    lax.fori_loop(0, nu, stage_own, 0)
-    for c in ins[1:]:
-        c.start()
-
     barrier = pltpu.get_barrier_semaphore()
     beside = [(lax.rem(q + k, NQ), t) for k in range(NQ) for t in (up, down)]
     partners = phases[0] + beside + phases[1]
     for p in partners:
         pl.semaphore_signal(barrier, inc=1, device_id=p, device_id_type=MESH)
+
+    base = pl.multiple_of(q * LANES, LANES)
+    own = pl.ds(base, LANES)
+    ins = [
+        pltpu.make_async_copy(depth_hbm, depth, in_sem.at[0]),
+        pltpu.make_async_copy(albedo_hbm, albedo, in_sem.at[1]),
+        pltpu.make_async_copy(mask_hbm, mask, in_sem.at[2]),
+        pltpu.make_async_copy(obs_hbm, obs_own, in_sem.at[3]),
+    ]
+    mine = pl.ds(pl.multiple_of(q * nl, nl), nl)
+
+    def block(t, u):
+        r = pl.ds(pl.multiple_of(u * UNIT, UNIT), UNIT)
+        return obs_hbm.at[:, r, pl.ds(pl.multiple_of(t * LANES, LANES), LANES)]
+
+    def stage(u, carry):
+        for j, t in enumerate(others):
+            pltpu.make_async_copy(block(t, u), staged.at[j, u], st_sem.at[j]).start()
+        return carry
+
+    def stage_own(u, carry):
+        pltpu.make_async_copy(block(q, u), obs_all.at[u, mine], st_sem.at[NQ - 1]).start()
+        return carry
+
+    for c in ins[:3]:
+        c.start()
+    lax.fori_loop(0, nu, stage, 0)
+    ins[3].start()
+    lax.fori_loop(0, nu, stage_own, 0)
 
     def ob_copy(j, u):
         t = others[j]
@@ -148,7 +149,7 @@
             c.start()
         return out
 
-    for k in (1, 2, 3):
+    for k in range(3):
         ins[k].wait()
     center = pl.ds(8, rows)
     spad[...] = jnp.zeros_like(spad)
@@ -160,10 +161,24 @@
         0, ((depth[:, own], True), (alb_own[...], False), (mask[:, own].astype(f32), False))
     )
 
-    ins[0].wait()
-    tables[pl.ds(q, 1)] = jnp.zeros((1, 4, LANES), f32)
-    tables[pl.ds(q, 1), :, 0:nl] = table[...].astype(f32)[None]
-    ins[4].wait()
+    for k in range(4):
+        row = jnp.zeros((1, LANES), f32)
+        for l in range(nl):
+            row = jnp.where(lane1 == l, table_ref[k, l].astype(f32), row)
+        tables[pl.ds(q, 1), k : k + 1, :] = row[None]
+    pl.semaphore_wait(barrier, len(partners))
+    tb = [
+        remote(tables.at[q], tables.at[q], tb_send.at[j], tb_recv.at[j], (t, s)) for j, t in enumerate(others)
+    ]
+    for c in tb:
+        c.start()
+
+    pk = send_edges(0)
+    for j in range(NQ - 1):
+        pltpu.make_async_copy(staged.at[j], staged.at[j], st_sem.at[j]).wait()
+    lax.fori_loop(0, AHEAD, send_obs, 0)
+
+    ins[3].wait()
     e_row = lax.broadcasted_iota(jnp.int32, (2 * NQ, COLS), 0)
     e_col = lax.broadcasted_iota(jnp.int32, (2 * NQ, COLS), 1)
     wanted = lax.rem((e_row // 2) * LANES + jnp.where(lax.rem(e_row, 2) == 0, COLS - 1, LANES), COLS)
@@ -174,14 +189,6 @@
         )
         for e in range(2 * NQ):
             edge_obs[e, l : l + 1, :] = got[e : e + 1]
-    pl.semaphore_wait(barrier, len(partners))
-    tb = [
-        remote(tables.at[q], tables.at[q], tb_send.at[j], tb_recv.at[j], (t, s)) for j, t in enumerate(others)
-    ]
-    for c in tb:
-        c.start()
-
-    pk = send_edges(0)
     eo = []
     for j, t in enumerate(others):
         for side in range(2):
@@ -199,9 +206,7 @@
     for c in eo + lo:
         c.start()
 
-    for j in range(NQ - 1):
-        pltpu.make_async_copy(staged.at[j], staged.at[j], st_sem.at[j]).wait()
-    lax.fori_loop(0, nu, send_obs, 0)
+    lax.fori_loop(AHEAD, nu, send_obs, 0)
 
     for c in tb:
         c.wait()
@@ -234,11 +239,13 @@
     py = coord_y(lax.broadcasted_iota(jnp.int32, (rows, LANES), 0))
     py_lane = coord_y(lane1)
     d = lx - px
-    dx2[...] = d * d
+    dx1[...] = d
 
     def make_c2(l, carry):
         dy = lights[1, pl.ds(l, 1), :] - py
-        c2[l] = dy * dy + dx2[pl.ds(l, 1), :]
+        dxr = dx1[pl.ds(l, 1), :]
+        dy1[l] = jnp.broadcast_to(dy, (rows, LANES))
+        c2[l] = dy * dy + dxr * dxr
         return carry
 
     lax.fori_loop(0, NL, make_c2, 0)
@@ -290,6 +297,11 @@
         )
         return to_rows(-(keep[side] * val * rn * alb / total) * inner)
 
+    def drain(u, carry):
+        for j in range(NQ - 1):
+            ob_copy(j, u).wait_send()
+        return carry
+
     sent, gathered = [], []
     for it in range(ITERS):
         last = it == ITERS - 1
@@ -300,11 +312,10 @@
         nsq = 1.0 + sx * sx + sy * sy
         rn = lax.rsqrt(nsq)
         pix[0] = surf
-        pix[1] = -surf + sx * px + sy * py
         pix[2] = sx
         pix[3] = sy
-        pix[4] = alb_own[...] * rn
-        pix[5] = mask[:, own].astype(f32) * rn
+        pix[4] = alb_own[...] * (rn * ROOT)
+        pix[5] = mask[:, own].astype(f32) * (rn / ROOT)
         pix[6] = rn * rn
         gx_lo, gx_hi = side_gradient(0), side_gradient(1)
 
@@ -313,38 +324,41 @@
             if it == 0:
                 for j in range(NQ - 1):
                     ob_copy(j, u).wait_recv()
-            sv, qv, sxv, syv, av = (pix[k, rs, :] for k in range(5))
+            sv, sxv, syv, av = (pix[k, rs, :] for k in (0, 2, 3, 4))
             low = None
             for l in range(NL):
                 ls = pl.ds(l, 1)
-                lxv, lyv, lzv, lev = (lights[k, ls, :] for k in range(4))
+                lzv, lev = lights[2, ls, :], lights[3, ls, :]
                 dz = lzv - sv
                 dist = dz * dz + c2[l, rs, :]
-                facing = (qv + lzv) - sxv * lxv - syv * lyv
+                facing = dz - sxv * dx1[ls, :] - syv * dy1[l, rs, :]
                 ri = lax.rsqrt(dist)
                 r2 = ri * ri
                 fall = lev * (r2 * ri)
                 fac = fall * facing
-                t = av * fac - obs_all[u, l].astype(f32)
+                if it == 0:
+                    seen = obs_all[u, l].astype(f32) * ROOT
+                    obs_f[u, l] = seen
+                else:
+                    seen = obs_f[u, l]
+                t = av * fac - seen
                 tt[l] = t
                 ff[l] = fall
                 fp[l] = fac
                 gg[l] = dz * r2
                 uu = t * t
                 low = uu if low is None else jnp.minimum(low, uu)
-            low = low * HALF_LOG2E
             acc = None
             for l in range(NL):
                 ls = pl.ds(l, 1)
                 t = tt[l]
-                p = jnp.exp2(low - HALF_LOG2E * (t * t))
+                p = jnp.exp2(low - t * t)
                 w = p * t
                 pull = w * ff[l]
                 pf = w * fp[l]
-                new = (p, pf, pf * gg[l], pull, pull * lights[0, ls, :], pull * lights[1, ls, :])
+                new = (p, pf, pf * gg[l], pull, pull * dx1[ls, :], pull * dy1[l, rs, :])
                 acc = new if acc is None else tuple(a + b for a, b in zip(acc, new))
             ssum, A, D, PU, X, Y = acc
-            pyv = py[0:UNIT] + lax.convert_element_type(u * UNIT, f32) / TOTAL
             scale = pix[5, rs, :] / ssum
             alb = alb_own[rs, :]
             ga = scale * A
@@ -352,8 +366,8 @@
             tilt = ga * alb * pix[6, rs, :]
             ga_all[it, rs, own] = ga
             gd[rs, :] = ca * (3.0 * D - PU)
-            gx[rs, :] = ca * (px * PU - X) - tilt * sxv
-            gypad[pl.ds(pl.multiple_of(u * UNIT + 8, 8), UNIT), :] = ca * (pyv * PU - Y) - tilt * syv
+            gx[rs, :] = -ca * X - tilt * sxv
+            gypad[pl.ds(pl.multiple_of(u * UNIT + 8, 8), UNIT), :] = -ca * Y - tilt * syv
             return carry
 
         lax.fori_loop(0, nu, unit, 0)
@@ -391,7 +405,11 @@
                     c.wait()
                 for c in onward:
                     c.start()
+                if not last:
+                    lax.fori_loop(0, nu, drain, 0)
                 if last:
+                    for w in sent[:-1]:
+                        w.wait_send()
                     for c in gathered:
                         c.wait()
                     depth[...] = depth[...] - step_depth * jnp.tanh(fd_all[0] * inv_d)
@@ -420,13 +438,7 @@
                 halo[side, 0:2, :] = keep[side] * (halo[side, 0:2, :] - step_depth * jnp.tanh(v[0:2] * inv_d))
                 halo[side, 2:3, :] = halo[side, 2:3, :] - step_albedo * jnp.tanh(v[2:3] * inv_a)
 
-    def drain(u, carry):
-        for j in range(NQ - 1):
-            ob_copy(j, u).wait_send()
-        return carry
-
-    lax.fori_loop(0, nu, drain, 0)
-    for w in sent:
+    for w in sent[-2:]:
         w.wait_send()
 
 
@@ -451,14 +463,15 @@
         return pl.pallas_call(
             functools.partial(kernel, cfg),
             out_shape=(out, out),
-            in_specs=[any_spec] * 5,
+            in_specs=[any_spec] * 3 + [pl.BlockSpec(memory_space=pltpu.SMEM), any_spec],
             out_specs=(vm, vm),
             scratch_shapes=[
-                V((rows, cols), f32), V((rows, cols), f32), V((rows, cols), jnp.int32), V((4, nl), jnp.int32),
+                V((rows, cols), f32), V((rows, cols), f32), V((rows, cols), jnp.int32),
                 V((nl, rows, cols), jnp.bfloat16), V((nu, NL, UNIT, LANES), jnp.bfloat16),
                 V((NQ, 4, LANES), f32), V((4, NL, LANES), f32),
                 V((NQ - 1, nu, nl, UNIT, LANES), jnp.bfloat16),
-                V((NL, LANES), f32), V((NL, rows, LANES), f32), V((rows + 16, LANES), f32), V((rows, LANES), f32),
+                V((NL, LANES), f32), V((NL, rows, LANES), f32), V((nu, NL, UNIT, LANES), f32),
+                V((NL, rows, LANES), f32), V((rows + 16, LANES), f32), V((rows, LANES), f32),
                 V((rows, LANES), f32), V((rows + 16, LANES), f32), V((rows, LANES), f32), V((7, rows, LANES), f32),
                 V((NL, UNIT, LANES), f32), V((NL, UNIT, LANES), f32),
                 V((NL, UNIT, LANES), f32), V((NL, UNIT, LANES), f32),
@@ -466,16 +479,16 @@
                 V((ITERS, 2, 8, LANES), f32), V((ITERS, 2, 8, LANES), f32), V((2, 8, LANES), f32),
                 V((ITERS, rows, cols), f32), V((ITERS, rows, cols), f32),
                 V((ITERS, NQ * FACT[2], 2, LANES), f32), V((ITERS, FACT[0] * FACT[1], 2, LANES), f32),
-                D((5,)), D((NQ,)), D((NQ - 1, nu)), D((NQ - 1, nu)), D((NQ - 1,)), D((NQ - 1,)),
+                D((4,)), D((NQ,)), D((NQ - 1, nu)), D((NQ - 1, nu)), D((NQ - 1,)), D((NQ - 1,)),
                 D((NQ - 1, 2)), D((NQ - 1, 2)), D((2,)), D((2,)),
                 D((ITERS, 2)), D((ITERS, 2)), D((ITERS, 3, 2)), D((ITERS, 3, 2)), D((ITERS, 2)), D((ITERS, 2)),
             ],
             compiler_params=pltpu.CompilerParams(
-                collective_id=0, has_side_effects=True, vmem_limit_bytes=56 * 2**20
+                collective_id=0, has_side_effects=True, vmem_limit_bytes=40 * 2**20
             ),
             cost_estimate=pl.CostEstimate(flops=10**8, bytes_accessed=3 * 2**20, transcendentals=10**6),
             name="steps",
-        )(depth, albedo, obs, table.T, mask)
+        )(*(pltpu.with_memory_space_constraint(v, pltpu.HBM) for v in (depth, albedo, obs, table.T, mask)))
 
     in_specs = (
         P(None, "strip"),

time: 59 us -> 57.4 us (0.973)
  local copies, waits for them, and re-layouts: 2.42 us -> 1.41 us
  Pallas kernels: 55.8 us -> 55.2 us
    unnamed x4 -> x2, local copies, waits for them, and re-layouts: 2.42 us -> 1.41 us
where the time goes in v4:
time: 57.4 us; the launch traced here: 57.3 us
  Pallas kernels  55.2 us (96%)
  local copies, waits for them, and re-layouts  1.41 us (2%)
  between operations  0.64 us (1%)
    pallas_call x1, Pallas kernels, shards(): pl.pallas_call(functools.partial(kernel, cfg), out_shape=(out, out), in_s...  55.2 us
    unnamed x2, local copies, waits for them, and re-layouts  1.41 us

profile of v4, /device:TPU:1, one launch (start us, length us, event | category | flops | bytes accessed | tf_op | source)
XLA Modules:
  0.0 57.3 jit_solution(1488423118028060019)
XLA Ops:
  0.6 55.2 %steps.1 = (f32[128,512]{1,0:T(8,128)S(1)}, f32[128,512]{1,0:T(8,128)S(1)}) custom-call(f32[128,512]{1,0:T(8,128)} %depth_hbm.1, f32[128,512]{1,0:T(8,128)} %albedo_hbm.1, bf16[8,128,512]{2,1,0:T(8,128)(2,1)} %obs_hbm.1, s32[4,8]{1,0:T(4,128)} %bitcast.1, s32[128,512]{1,0:T(8,128)} %mask_hbm.1), custom_call_target="tpu_custom_call" | custom-call | flops 100000000 | bytes 3145728 | tf_op jit(solution)/shard_map/steps/pallas_call | solution.py:463
  55.9 0.7 %copy.9 = f32[128,512]{1,0:T(8,128)} copy(f32[128,512]{1,0:T(8,128)S(1)} %get-tuple-element.4) | data formatting | bytes 524288
  56.6 0.7 %copy.10 = f32[128,512]{1,0:T(8,128)} copy(f32[128,512]{1,0:T(8,128)S(1)} %get-tuple-element.5) | data formatting | bytes 524288

commit v5 on v4

--- a/solution.py
+++ b/solution.py
@@ -442,6 +442,17 @@
         w.wait_send()
 
 
+def write_out(depth_in, albedo_in, depth_hbm, albedo_hbm, sem):
+    copies = [
+        pltpu.make_async_copy(depth_in, depth_hbm, sem.at[0]),
+        pltpu.make_async_copy(albedo_in, albedo_hbm, sem.at[1]),
+    ]
+    for c in copies:
+        c.start()
+    for c in copies:
+        c.wait()
+
+
 def factors(n):
     return {128: (8, 8, 2)}[n]
 
@@ -460,7 +471,7 @@
         any_spec = pl.BlockSpec(memory_space=pl.ANY)
         vm = pl.BlockSpec(memory_space=pltpu.VMEM)
         out = jax.ShapeDtypeStruct((rows, cols), f32)
-        return pl.pallas_call(
+        results = pl.pallas_call(
             functools.partial(kernel, cfg),
             out_shape=(out, out),
             in_specs=[any_spec] * 3 + [pl.BlockSpec(memory_space=pltpu.SMEM), any_spec],
@@ -489,6 +500,15 @@
             cost_estimate=pl.CostEstimate(flops=10**8, bytes_accessed=3 * 2**20, transcendentals=10**6),
             name="steps",
         )(*(pltpu.with_memory_space_constraint(v, pltpu.HBM) for v in (depth, albedo, obs, table.T, mask)))
+        return pl.pallas_call(
+            write_out,
+            out_shape=(out, out),
+            in_specs=[vm, vm],
+            out_specs=(pl.BlockSpec(memory_space=pltpu.HBM),) * 2,
+            scratch_shapes=[D((2,))],
+            compiler_params=pltpu.CompilerParams(vmem_limit_bytes=16 * 2**20),
+            name="write_out",
+        )(*results)
 
     in_specs = (
         P(None, "strip"),

time: 57.4 us -> 56.8 us (0.990)
  local copies, waits for them, and re-layouts: 1.41 us -> 0 us
  Pallas kernels: 55.2 us -> 56 us
    unnamed x2 -> x0, local copies, waits for them, and re-layouts: 1.41 us -> none
    pallas_call x0 -> x1, Pallas kernels: none -> 0.81 us  [shards(): pl.pallas_call(write_out, out_shape=(out, out), in_specs=[vm, vm], out_sp...]
where the time goes in v5:
time: 56.8 us; the launch traced here: 56.7 us
  Pallas kernels  56 us (99%)
  between operations  0.64 us (1%)
    pallas_call x1, Pallas kernels, shards(): pl.pallas_call(functools.partial(kernel, cfg), out_shape=(out, out), in_s...  55.2 us

profile of v5, /device:TPU:1, one launch (start us, length us, event | category | flops | bytes accessed | tf_op | source)
XLA Modules:
  0.0 56.7 jit_solution(9499762045715239684)
XLA Ops:
  0.6 55.2 %steps.1 = (f32[128,512]{1,0:T(8,128)S(1)}, f32[128,512]{1,0:T(8,128)S(1)}) custom-call(f32[128,512]{1,0:T(8,128)} %depth_hbm.1, f32[128,512]{1,0:T(8,128)} %albedo_hbm.1, bf16[8,128,512]{2,1,0:T(8,128)(2,1)} %obs_hbm.1, s32[4,8]{1,0:T(4,128)} %bitcast.1, s32[128,512]{1,0:T(8,128)} %mask_hbm.1), custom_call_target="tpu_custom_call" | custom-call | flops 100000000 | bytes 3145728 | tf_op jit(solution)/shard_map/steps/pallas_call | solution.py:474
  55.9 0.8 %write_out.1 = (f32[128,512]{1,0:T(8,128)}, f32[128,512]{1,0:T(8,128)}) custom-call(f32[128,512]{1,0:T(8,128)S(1)} %get-tuple-element.4.depth_in, f32[128,512]{1,0:T(8,128)S(1)} %get-tuple-element.5.albedo_in), custom_call_target="tpu_custom_call" | custom-call | tf_op jit(solution)/shard_map/write_out/pallas_call | solution.py:503

commit v6 on v5

--- a/solution.py
+++ b/solution.py
@@ -32,7 +32,7 @@
     depth_hbm, albedo_hbm, obs_hbm, table_ref, mask_hbm,
     depth_out, albedo_out,
     depth, albedo, mask, obs_own, obs_all, tables, lights,
-    staged, dx1, dy1, obs_f, c2, spad, alb_own, gx, gypad, gd, pix,
+    dx1, dy1, obs_f, c2, spad, alb_own, gx, gypad, gd, pix,
     tt, ff, fp, gg,
     edge_obs, halo_obs, halo_loop, pack_out, pack_in, halo,
     fd_all, ga_all, near_sums, far_sums,
@@ -74,7 +74,8 @@
     counts = [NQ * nx, nz * ny]
 
     barrier = pltpu.get_barrier_semaphore()
-    beside = [(lax.rem(q + k, NQ), t) for k in range(NQ) for t in (up, down)]
+    other = jnp.where(xh == 0, down, up)
+    beside = [(lax.rem(q + k, NQ), other) for k in range(NQ)]
     partners = phases[0] + beside + phases[1]
     for p in partners:
         pl.semaphore_signal(barrier, inc=1, device_id=p, device_id_type=MESH)
@@ -93,25 +94,19 @@
         r = pl.ds(pl.multiple_of(u * UNIT, UNIT), UNIT)
         return obs_hbm.at[:, r, pl.ds(pl.multiple_of(t * LANES, LANES), LANES)]
 
-    def stage(u, carry):
-        for j, t in enumerate(others):
-            pltpu.make_async_copy(block(t, u), staged.at[j, u], st_sem.at[j]).start()
-        return carry
-
     def stage_own(u, carry):
-        pltpu.make_async_copy(block(q, u), obs_all.at[u, mine], st_sem.at[NQ - 1]).start()
+        pltpu.make_async_copy(block(q, u), obs_all.at[u, mine], st_sem.at[0]).start()
         return carry
 
     for c in ins[:3]:
         c.start()
-    lax.fori_loop(0, nu, stage, 0)
     ins[3].start()
     lax.fori_loop(0, nu, stage_own, 0)
 
     def ob_copy(j, u):
         t = others[j]
         return remote(
-            staged.at[j, u], obs_all.at[u, mine], ob_send.at[j, u], ob_recv.at[j, u], (t, s)
+            block(others[j], u), obs_all.at[u, mine], ob_send.at[j, u], ob_recv.at[j, u], (t, s)
         )
 
     def send_obs(u, carry):
@@ -174,8 +169,6 @@
         c.start()
 
     pk = send_edges(0)
-    for j in range(NQ - 1):
-        pltpu.make_async_copy(staged.at[j], staged.at[j], st_sem.at[j]).wait()
     lax.fori_loop(0, AHEAD, send_obs, 0)
 
     ins[3].wait()
@@ -263,7 +256,7 @@
         v = pack_in[0, side]
         halo[side, 0:2, :] = v[0:2] * keep[side]
         halo[side, 2:4, :] = v[2:4]
-    pltpu.make_async_copy(obs_all.at[:, mine], obs_all.at[:, mine], st_sem.at[NQ - 1]).wait()
+    pltpu.make_async_copy(obs_all.at[:, mine], obs_all.at[:, mine], st_sem.at[0]).wait()
 
     def widen(v, lo_col, hi_col):
         lo_v = jnp.where(lane == 0, lo_col, pltpu.roll(v, 1, 1))
@@ -317,7 +310,8 @@
         pix[4] = alb_own[...] * (rn * ROOT)
         pix[5] = mask[:, own].astype(f32) * (rn / ROOT)
         pix[6] = rn * rn
-        gx_lo, gx_hi = side_gradient(0), side_gradient(1)
+        if it == 0:
+            gx_lo, gx_hi = side_gradient(0), side_gradient(1)
 
         def unit(u, carry):
             rs = pl.ds(pl.multiple_of(u * UNIT, UNIT), UNIT)
@@ -370,7 +364,12 @@
             gypad[pl.ds(pl.multiple_of(u * UNIT + 8, 8), UNIT), :] = -ca * Y - tilt * syv
             return carry
 
-        lax.fori_loop(0, nu, unit, 0)
+        if it == 0:
+            lax.fori_loop(0, nu, unit, 0)
+        else:
+            lax.fori_loop(0, nu - 1, unit, 0)
+            gx_lo, gx_hi = side_gradient(0), side_gradient(1)
+            unit(nu - 1, 0)
         lo_v, hi_v = widen(gx[...], gx_lo, gx_hi)
         fd = gd[...] + 0.5 * (lo_v - hi_v) + 0.5 * (gypad[pl.ds(7, rows), :] - gypad[pl.ds(9, rows), :])
         ga = ga_all[it, :, own]
@@ -480,7 +479,6 @@
                 V((rows, cols), f32), V((rows, cols), f32), V((rows, cols), jnp.int32),
                 V((nl, rows, cols), jnp.bfloat16), V((nu, NL, UNIT, LANES), jnp.bfloat16),
                 V((NQ, 4, LANES), f32), V((4, NL, LANES), f32),
-                V((NQ - 1, nu, nl, UNIT, LANES), jnp.bfloat16),
                 V((NL, LANES), f32), V((NL, rows, LANES), f32), V((nu, NL, UNIT, LANES), f32),
                 V((NL, rows, LANES), f32), V((rows + 16, LANES), f32), V((rows, LANES), f32),
                 V((rows, LANES), f32), V((rows + 16, LANES), f32), V((rows, LANES), f32), V((7, rows, LANES), f32),
@@ -490,7 +488,7 @@
                 V((ITERS, 2, 8, LANES), f32), V((ITERS, 2, 8, LANES), f32), V((2, 8, LANES), f32),
                 V((ITERS, rows, cols), f32), V((ITERS, rows, cols), f32),
                 V((ITERS, NQ * FACT[2], 2, LANES), f32), V((ITERS, FACT[0] * FACT[1], 2, LANES), f32),
-                D((4,)), D((NQ,)), D((NQ - 1, nu)), D((NQ - 1, nu)), D((NQ - 1,)), D((NQ - 1,)),
+                D((4,)), D((1,)), D((NQ - 1, nu)), D((NQ - 1, nu)), D((NQ - 1,)), D((NQ - 1,)),
                 D((NQ - 1, 2)), D((NQ - 1, 2)), D((2,)), D((2,)),
                 D((ITERS, 2)), D((ITERS, 2)), D((ITERS, 3, 2)), D((ITERS, 3, 2)), D((ITERS, 2)), D((ITERS, 2)),
             ],

time: 56.8 us -> 56.9 us (level)
  no operation moved by 1% of the time
where the time goes in v6:
time: 56.9 us; the launch traced here: 56.8 us
  Pallas kernels  56.1 us (99%)
  between operations  0.64 us (1%)
    pallas_call x1, Pallas kernels, shards(): pl.pallas_call(functools.partial(kernel, cfg), out_shape=(out, out), in_s...  55.3 us

profile of v6, /device:TPU:1, one launch (start us, length us, event | category | flops | bytes accessed | tf_op | source)
XLA Modules:
  0.0 56.8 jit_solution(13722017599996795055)
XLA Ops:
  0.6 55.3 %steps.1 = (f32[128,512]{1,0:T(8,128)S(1)}, f32[128,512]{1,0:T(8,128)S(1)}) custom-call(f32[128,512]{1,0:T(8,128)} %depth_hbm.1, f32[128,512]{1,0:T(8,128)} %albedo_hbm.1, bf16[8,128,512]{2,1,0:T(8,128)(2,1)} %obs_hbm.1, s32[4,8]{1,0:T(4,128)} %bitcast.1, s32[128,512]{1,0:T(8,128)} %mask_hbm.1), custom_call_target="tpu_custom_call" | custom-call | flops 100000000 | bytes 3145728 | tf_op jit(solution)/shard_map/steps/pallas_call | solution.py:473
  56.0 0.8 %write_out.1 = (f32[128,512]{1,0:T(8,128)}, f32[128,512]{1,0:T(8,128)}) custom-call(f32[128,512]{1,0:T(8,128)S(1)} %get-tuple-element.4.depth_in, f32[128,512]{1,0:T(8,128)S(1)} %get-tuple-element.5.albedo_in), custom_call_target="tpu_custom_call" | custom-call | tf_op jit(solution)/shard_map/write_out/pallas_call | solution.py:501
